TPU v7x, 256 devices: a whole 4x4x8 slice. The times are simulated.
256 devices in a mesh: fsdp: 32 (over x_lo, z, core), ctx: 8 (over y, x_hi).
Axes of the slice: x: 4 (x_hi: 2, x_lo: 2; x = x_hi * 2 + x_lo), y: 4, z: 8, core: 2. Of those that a mesh axis runs over, the one named last changes fastest.
Arguments:
- tokens: bfloat16 [32, 4096, 4096], P('fsdp', 'ctx'), may hold values from -24 to 24
- w_query: bfloat16 [4096, 2, 128], P('fsdp'), may hold values from -0.09375 to 0.09375
- w_key: bfloat16 [4096, 2, 128], P('fsdp'), may hold values from -0.09375 to 0.09375
- w_value: bfloat16 [4096, 2, 4, 128], P('fsdp'), may hold values from -0.09375 to 0.09375
- w_out: bfloat16 [2, 4, 128, 4096], P(None, None, None, 'fsdp'), may hold values from -0.5 to 0.5
- value_experts: int32 [32, 4096, 2, 2], P('fsdp', 'ctx'), may hold values from 0 to 3, all different within a row
- value_gates: bfloat16 [32, 4096, 2, 2], P('fsdp', 'ctx'), may hold values from 0.25 to 1
- output_experts: int32 [32, 4096, 2, 2], P('fsdp', 'ctx'), may hold values from 0 to 3, all different within a row
- output_gates: bfloat16 [32, 4096, 2, 2], P('fsdp', 'ctx'), may hold values from 0.25 to 1
Outputs:
- projected: bfloat16 [32, 4096, 4096], P('fsdp', 'ctx')
Inputs may be any that keep to these rules, and one draw needn't show every extreme that they name: `value_experts`: each token and head names 2 different experts. `output_experts`: each token and head names 2 different experts.
All inputs are finite; a program needn't handle non-finite values.
Results may differ from a plain program's by a relative error of at most 0.015.
The roundings to bfloat16 on the way count: a program that leaves them out, or rounds other values in their place, can miss the bound.
Values may be sent and summed in bfloat16 or wider, within the bound.
No kernel may reach another device: no remote copies, remote signals or barrier semaphores. Data moves between devices by JAX's collectives and lax.ppermute only.
A program may use at most 128 MiB of HBM per device.

v0:
```python
import functools
import itertools
import math

import jax
import jax.numpy as jnp
from jax import lax
from jax.experimental import pallas as pl
from jax.experimental.pallas import tpu as pltpu
from jax.sharding import Mesh
from jax.sharding import PartitionSpec as P

AXES = ("x_lo", "z", "core", "y", "x_hi")
SIZES = (2, 8, 2, 4, 2)
FSDP = ("x_lo", "z", "core")
CTX = ("y", "x_hi")
HEADS, EXPERTS, DH = 2, 4, 128
WIDTH = HEADS * DH
MIB = 1 << 20


def expert_mix(indices, gates):
    one_hot = (indices[..., None] == jnp.arange(EXPERTS, dtype=jnp.int32)).astype(jnp.float32)
    mix = jnp.sum(gates.astype(jnp.float32)[..., None] * one_hot, axis=-2)
    return mix.reshape(mix.shape[0], HEADS * EXPERTS).T


RING = 4
VM = pltpu.CompilerParams(vmem_limit_bytes=60 * MIB)


def moved(x, target):
    pairs = []
    for source, (x_lo, z, core, y, x_hi) in enumerate(itertools.product(*map(range, SIZES))):
        to_x, to_y, to_core = target(2 * x_hi + x_lo, y, core)
        to_x, to_y = to_x % RING, to_y % RING
        place = (((to_x % 2) * SIZES[1] + z) * SIZES[2] + to_core) * SIZES[3] + to_y
        pairs.append((source, place * SIZES[4] + to_x // 2))
    return lax.ppermute(x, AXES, pairs)


def hop(x, by, phase):
    return moved(
        x, lambda cx, cy, core: (cx + by, cy, core) if core == phase else (cx, cy + by, core)
    )


def swapped(x):
    return lax.ppermute(x, "core", [(0, 1), (1, 0)])


FIRST = ((0, -1), (1, 2))
GROUPS = ((0, 0), (0, 1), (-1, 0), (1, 1), (1, 0), (-1, 1), (2, 0), (2, 1))


def lifted(x):
    pairs = []
    for source, (x_lo, z, core, y, x_hi) in enumerate(itertools.product(*map(range, SIZES))):
        by = y * SIZES[4] + x_hi
        to_z = (z + by if core == 0 else z - by) % SIZES[1]
        place = ((x_lo * SIZES[1] + to_z) * SIZES[2] + core) * SIZES[3] + y
        pairs.append((source, place * SIZES[4] + x_hi))
    return lax.ppermute(x, AXES, pairs)


def gathered(block):
    up = hop(block, 1, 0)
    down = hop(block, -1, 0)
    across = hop(block, 2, 0)
    near = jnp.stack([block, up])
    far = jnp.stack([down, across])
    near_up = hop(near, 1, 1)
    far_down = hop(far, -1, 1)
    near_down = hop(near, -1, 1)
    far_up = hop(far, 1, 1)
    near_across = hop(near_up, 1, 1)
    far_across = hop(far_down, -1, 1)
    return [near, far, near_up, far_down, near_down, far_up, near_across, far_across]


def pack_kernel(place_ref, own_ref, other_ref, out_ref):
    rows = own_ref.shape[0]
    core = place_ref[3]
    for i in range(SIZES[0] * SIZES[1]):
        lanes = pl.ds(pl.multiple_of((SIZES[2] * i + core) * DH, DH), DH)
        out_ref[:rows, i * DH : (i + 1) * DH] = own_ref[:, lanes]
        out_ref[rows:, i * DH : (i + 1) * DH] = other_ref[:, lanes]


def packed(place, own, other):
    rows, depth = own.shape
    vmem = pl.BlockSpec(memory_space=pltpu.VMEM)
    return pl.pallas_call(
        pack_kernel,
        in_specs=[pl.BlockSpec(memory_space=pltpu.SMEM), vmem, vmem],
        out_specs=vmem,
        out_shape=jax.ShapeDtypeStruct((2 * rows, depth // 2), own.dtype),
        compiler_params=VM,
        cost_estimate=pl.CostEstimate(
            flops=0, bytes_accessed=6 * rows * depth, transcendentals=0
        ),
    )(place, own, other)


HALVES = ((0, 512), (512, 768))


def project_kernel(count, place_ref, x_hbm, mix_ref, far_mix_ref, *refs):
    pieces = refs[:count]
    own_ref, other_ref, x_ref, w_ref, x_sem, w_sem = refs[count:]
    chip_x, chip_y, level, core = (place_ref[i] for i in range(4))
    rows = own_ref.shape[0]
    x_copy = pltpu.make_async_copy(x_hbm, x_ref, x_sem)
    w_copies = [[] for _ in HALVES]
    for i, piece in enumerate(pieces):
        second, pair = GROUPS[i]
        for j, first in enumerate(FIRST[pair]):
            by_x = jnp.where(core == 0, first, second)
            by_y = jnp.where(core == 0, second, first)
            from_x = lax.rem(chip_x + by_x + RING, RING)
            from_y = lax.rem(chip_y + by_y + RING, RING)
            by = from_y * SIZES[4] + lax.div(from_x, 2)
            from_z = lax.rem(level + jnp.where(core == 0, SIZES[1] - by, by), SIZES[1])
            shard = lax.rem(from_x, 2) * SIZES[1] + from_z
            for h, (start, size) in enumerate(HALVES):
                columns = pl.ds(start, size)
                w_copies[h].append(
                    pltpu.make_async_copy(
                        piece.at[j, :, columns], w_ref.at[shard, :, columns], w_sem.at[h]
                    )
                )
    for copy in w_copies[0]:
        copy.start()
    x_copy.start()
    for copy in w_copies[1]:
        copy.start()
    mixes = (jnp.transpose(mix_ref[...]), jnp.transpose(far_mix_ref[...]))
    x_copy.wait()
    for copy in w_copies[0]:
        copy.wait()

    def product(column):
        w = w_ref[:, :, column : column + WIDTH].reshape(x_ref.shape[1], WIDTH)
        block = jnp.dot(x_ref[...], w, preferred_element_type=jnp.float32)
        return block[:rows], block[rows:]

    outs = (own_ref, other_ref)
    for out, block in zip(outs, product(0)):
        out[:, :WIDTH] = block
    for head in range(HEADS):
        for half in range(EXPERTS // 2):
            if head == 0 and half == 1:
                for copy in w_copies[1]:
                    copy.wait()
            expert = head * EXPERTS + 2 * half
            lanes = slice(WIDTH + head * DH, WIDTH + (head + 1) * DH)
            for out, mix, block in zip(outs, mixes, product(WIDTH + expert * DH)):
                part = (
                    mix[:, expert : expert + 1] * block[:, :DH]
                    + mix[:, expert + 1 : expert + 2] * block[:, DH:]
                )
                out[:, lanes] = part if half == 0 else out[:, lanes] + part


def project(place, x, mix, far_mix, pieces):
    rows = x.shape[0] // 2
    depth = x.shape[1]
    _, shard, columns = pieces[0].shape
    any_space = pl.BlockSpec(memory_space=pl.ANY)
    vmem = pl.BlockSpec(memory_space=pltpu.VMEM)
    count = len(pieces)
    return pl.pallas_call(
        functools.partial(project_kernel, count),
        in_specs=[pl.BlockSpec(memory_space=pltpu.SMEM), any_space, vmem, vmem]
        + [any_space] * count,
        out_specs=[vmem, vmem],
        out_shape=[jax.ShapeDtypeStruct((rows, 2 * WIDTH), jnp.float32)] * 2,
        scratch_shapes=[
            pltpu.VMEM(x.shape, x.dtype),
            pltpu.VMEM((2 * count, shard, columns), jnp.bfloat16),
            pltpu.SemaphoreType.DMA,
            pltpu.SemaphoreType.DMA((len(HALVES),)),
        ],
        compiler_params=VM,
        cost_estimate=pl.CostEstimate(
            flops=4 * rows * depth * columns,
            bytes_accessed=2 * depth * (2 * rows + columns),
            transcendentals=0,
        ),
    )(place, x, mix, far_mix, *pieces)


def query_kernel(x_ref, w_ref, q_ref, acc_ref):
    n = pl.program_id(0)
    count = w_ref.shape[0]
    w = jnp.concatenate(
        [
            jnp.concatenate([w_ref[i, :DH], w_ref[i, DH:]], axis=1)
            for i in range(count)
        ],
        axis=0,
    )
    part = jnp.dot(x_ref[...], w, preferred_element_type=jnp.float32)

    @pl.when(n == 0)
    def _():
        acc_ref[...] = part

    @pl.when(n > 0)
    def _():
        acc_ref[...] += part

    @pl.when(n == pl.num_programs(0) - 1)
    def _():
        q_ref[...] = acc_ref[...].astype(jnp.bfloat16)


def query(x, panels):
    rows, depth = x.shape
    shards = panels.shape[0] * panels.shape[1]
    steps = 4
    return pl.pallas_call(
        query_kernel,
        grid=(steps,),
        in_specs=[
            pl.BlockSpec((rows, depth // steps), lambda n: (0, n)),
            pl.BlockSpec((shards // steps, None, WIDTH, DH), lambda n: (n % 2, n // 2, 4, 0)),
        ],
        out_specs=pl.BlockSpec((rows, WIDTH), lambda n: (0, 0)),
        out_shape=jax.ShapeDtypeStruct((rows, WIDTH), jnp.bfloat16),
        scratch_shapes=[pltpu.VMEM((rows, WIDTH), jnp.float32)],
        compiler_params=VM,
        cost_estimate=pl.CostEstimate(
            flops=2 * rows * depth * WIDTH,
            bytes_accessed=2 * (rows * depth + depth * WIDTH),
            transcendentals=0,
        ),
    )(x, panels)


LOG2E = 1.4426950408889634
PANELS = 4


def attend_block(q_ref, kv, m_ref, l_ref, acc_ref, diagonal):
    scale = LOG2E / math.sqrt(DH)
    for head in range(HEADS):
        lanes = slice(head * DH, (head + 1) * DH)
        one = slice(head, head + 1)
        scores = lax.dot_general(
            kv[:, lanes],
            q_ref[:, lanes],
            (((1,), (1,)), ((), ())),
            preferred_element_type=jnp.float32,
        )
        values = kv[:, WIDTH + head * DH : WIDTH + (head + 1) * DH]
        if diagonal:
            k_pos = lax.broadcasted_iota(jnp.int32, scores.shape, 0)
            q_pos = lax.broadcasted_iota(jnp.int32, scores.shape, 1)
            scores = jnp.where(q_pos >= k_pos, scores, -jnp.inf)
            top = jnp.max(scores, axis=0, keepdims=True)
        else:
            before = m_ref[one]
            top = jnp.maximum(before, jnp.max(scores, axis=0, keepdims=True))
            rescale = jnp.exp2((before - top) * scale)
        weights = jnp.exp2((scores - top) * scale)
        total = jnp.sum(weights, axis=0, keepdims=True)
        update = lax.dot_general(
            values,
            weights.astype(jnp.bfloat16),
            (((0,), (0,)), ((), ())),
            preferred_element_type=jnp.float32,
        )
        m_ref[one] = top
        if diagonal:
            l_ref[one] = total
            acc_ref[lanes] = update
        else:
            l_ref[one] = l_ref[one] * rescale + total
            acc_ref[lanes] = acc_ref[lanes] * rescale + update


def attend_blocks(place_ref, needs, diagonal, q_ref, kv_refs, *state):
    row, side = place_ref[1], lax.div(place_ref[0], 2)
    for k, kv in enumerate(kv_refs):
        if diagonal and k == 0:
            attend_block(q_ref, kv, *state, True)
        else:
            pl.when((row >= needs[k][0]) & (side >= needs[k][1]))(
                functools.partial(attend_block, q_ref, kv, *state, False)
            )


def attend_early_kernel(needs, place_ref, q_ref, *refs):
    count = len(needs)
    attend_blocks(place_ref, needs, True, q_ref, refs[:count], *refs[count:])


def attend_late_kernel(needs, place_ref, q_ref, m_in, l_in, acc_in, mix_ref, panels, *refs):
    count = len(needs)
    out_hbm = refs[count]
    m_ref, l_ref, acc_ref, mixed_ref, w_ref, o_ref, w_sem, o_sem = refs[count + 1 :]
    depth = mixed_ref.shape[1]
    levels, lows = panels.shape[:2]
    w_copies = [
        pltpu.make_async_copy(
            panels.at[pl.ds(first, PANELS), low, pl.ds(0, depth)],
            w_ref.at[pl.ds(low * levels + first, PANELS)],
            w_sem,
        )
        for low in range(lows)
        for first in range(0, levels, PANELS)
    ]
    for copy in w_copies:
        copy.start()
    m_ref[...] = m_in[...]
    l_ref[...] = l_in[...]
    acc_ref[...] = acc_in[...]
    attend_blocks(place_ref, needs, False, q_ref, refs[:count], m_ref, l_ref, acc_ref)
    mix = jnp.transpose(mix_ref[...])
    for head in range(HEADS):
        attended = acc_ref[head * DH : (head + 1) * DH] / l_ref[head : head + 1]
        attended = jnp.transpose(attended).astype(jnp.bfloat16).astype(jnp.float32)
        for expert in range(EXPERTS):
            index = head * EXPERTS + expert
            mixed_ref[:, index * DH : (index + 1) * DH] = (
                mix[:, index : index + 1] * attended
            ).astype(jnp.bfloat16)
    for copy in w_copies:
        copy.wait()
    o_copies = []
    width = 2 * DH
    for i in range(0, levels * lows, 2):
        panel = jnp.concatenate([w_ref[i], w_ref[i + 1]], axis=1)
        block = jnp.dot(mixed_ref[...], panel, preferred_element_type=jnp.float32)
        o_ref[:, i * DH : i * DH + width] = block.astype(jnp.bfloat16)
        if i % PANELS == PANELS - 2:
            lanes = pl.ds((i + 2 - PANELS) * DH, PANELS * DH)
            o_copies.append(
                pltpu.make_async_copy(o_ref.at[:, lanes], out_hbm.at[:, lanes], o_sem)
            )
            o_copies[-1].start()
    for copy in o_copies:
        copy.wait()


def state_shapes(rows):
    return [(HEADS, rows), (HEADS, rows), (WIDTH, rows)]


def attend_cost(rows, count, flops):
    return pl.CostEstimate(
        flops=4 * rows * rows * DH * HEADS * count + flops,
        bytes_accessed=2 * rows * WIDTH * 2 * count,
        transcendentals=rows * rows * HEADS * count,
    )


def attend_early(place, q, blocks, needs):
    rows = q.shape[0]
    vmem = pl.BlockSpec(memory_space=pltpu.VMEM)
    return pl.pallas_call(
        functools.partial(attend_early_kernel, needs),
        in_specs=[pl.BlockSpec(memory_space=pltpu.SMEM)] + [vmem] * (1 + len(blocks)),
        out_specs=[vmem] * 3,
        out_shape=[jax.ShapeDtypeStruct(s, jnp.float32) for s in state_shapes(rows)],
        compiler_params=VM,
        cost_estimate=attend_cost(rows, len(blocks), 0),
    )(place, q, *blocks)


def attend_late(place, q, state, mix, panels, blocks, needs):
    rows = q.shape[0]
    depth = HEADS * EXPERTS * DH
    levels, lows, _, width = panels.shape
    columns = levels * lows * width
    vmem = pl.BlockSpec(memory_space=pltpu.VMEM)
    any_space = pl.BlockSpec(memory_space=pl.ANY)
    return pl.pallas_call(
        functools.partial(attend_late_kernel, needs),
        in_specs=[pl.BlockSpec(memory_space=pltpu.SMEM)]
        + [vmem] * 5
        + [any_space]
        + [vmem] * len(blocks),
        out_specs=any_space,
        out_shape=jax.ShapeDtypeStruct((rows, columns), jnp.bfloat16),
        scratch_shapes=[pltpu.VMEM(s, jnp.float32) for s in state_shapes(rows)]
        + [
            pltpu.VMEM((rows, depth), jnp.bfloat16),
            pltpu.VMEM((levels * lows, depth, width), jnp.bfloat16),
            pltpu.VMEM((rows, columns), jnp.bfloat16),
            pltpu.SemaphoreType.DMA,
            pltpu.SemaphoreType.DMA,
        ],
        compiler_params=VM,
        cost_estimate=attend_cost(rows, len(blocks), 2 * rows * depth * columns),
    )(place, q, *state, mix, panels, *blocks)


def on_device(
    tokens, w_query, w_key, w_value, w_out, value_experts, value_gates, output_experts, output_gates
):
    x = tokens[0]
    y, x_hi = lax.axis_index("y"), lax.axis_index("x_hi")
    chip_x = 2 * x_hi + lax.axis_index("x_lo")
    place = jnp.stack([chip_x, y, lax.axis_index("z"), lax.axis_index("core")]).astype(jnp.int32)
    shard = w_key.shape[0]
    block = lifted(
        jnp.concatenate([w_key.reshape(shard, -1), w_value.reshape(shard, -1)], axis=1)
    )
    value_mix = expert_mix(value_experts[0], value_gates[0])
    output_mix = expert_mix(output_experts[0], output_gates[0])
    output_mix = output_mix.astype(jnp.bfloat16).astype(jnp.float32)
    panel = jnp.concatenate(
        [
            w_out.reshape(-1, w_out.shape[3]),
            jnp.transpose(w_query, (1, 0, 2)).reshape(-1, DH),
        ],
        axis=0,
    )
    across = lax.ppermute(panel, "x_lo", [(0, 1), (1, 0)])
    far_mix = swapped(value_mix)
    both = packed(place, x, swapped(x))
    block, across = lax.optimization_barrier((block, across))
    low = lax.axis_index("x_lo") == 0
    pair = jnp.stack([jnp.where(low, panel, across), jnp.where(low, across, panel)])
    panels = lax.all_gather(pair, ("z", "core"), axis=0, tiled=False)
    mine, theirs = project(place, both, value_mix, far_mix, gathered(block))
    own = (mine + swapped(theirs)).astype(jnp.bfloat16)
    q = query(x, panels)

    other = lax.ppermute(own, "x_hi", [(0, 1), (1, 0)])
    own_1 = lax.ppermute(own, "y", [(0, 1), (1, 2), (2, 3)])
    own_3 = lax.ppermute(own, "y", [(0, 3)])
    own_2 = lax.ppermute(own, "y", [(0, 2), (1, 3)])
    other_1 = lax.ppermute(other, "y", [(0, 1), (1, 2), (2, 3)])
    other_3 = lax.ppermute(other, "y", [(0, 3)])
    other_2 = lax.ppermute(own_2, "x_hi", [(0, 1), (1, 0)])
    state = attend_early(
        place, q, [own, other, own_1, own_2, own_3], ((0, 0), (0, 1), (1, 0), (2, 0), (3, 0))
    )
    result = attend_late(
        place,
        q,
        state,
        output_mix,
        panels,
        [other_1, other_2, other_3],
        ((1, 0), (2, 0), (3, 0)),
    )
    return result[None]


def solution(mesh):
    grid = Mesh(mesh.devices.reshape(SIZES), AXES)
    seq = P(FSDP, CTX, None, None)
    in_specs = (
        P(FSDP, CTX, None),
        P(FSDP, None, None),
        P(FSDP, None, None),
        P(FSDP, None, None, None),
        P(None, None, None, FSDP),
        seq,
        seq,
        seq,
        seq,
    )
    return jax.shard_map(
        on_device, mesh=grid, in_specs=in_specs, out_specs=P(FSDP, CTX, None), check_vma=False
    )
```

profile of v0, /device:TPU:54, one launch (start us, length us, event | category | flops | bytes accessed | tf_op | source)
XLA Modules:
  0.0 151.2 jit_solution(5002315964387457802)
XLA Ops:
  6.5 0.9 copy.24
  7.4 1.0 pad_maximum_fusion.3
  8.4 0.9 collective-permute-start.1
  9.3 1.1 reshape.38
  10.4 0.9 copy.27
  11.3 7.8 %collective-permute-start = (bf16[128,1280]{1,0:T(8,128)(2,1)S(1)}, bf16[128,1280]{1,0:T(8,128)(2,1)S(1)}, u32[]{:S(2)}, u32[]{:S(2)}) collective-permute-start(bf16[128,1280]{1,0:T(8,128)(2,1)S(1)} %pad_maximum_fusion.4), channel_id=1, source_target_pairs={{0,0},{1,17},{2,34},{3,51},{4,68},{5,85},{6,102},{7,119},{8,8},{9,... | collective-permute-start | bytes 983048 | tf_op jit(solution)/shard_map/ppermute | solution.py:63
  19.1 0.0 collective-permute-done.1
  19.1 9.1 %collective-permute-done = bf16[128,1280]{1,0:T(8,128)(2,1)S(1)} collective-permute-done((bf16[128,1280]{1,0:T(8,128)(2,1)S(1)}, bf16[128,1280]{1,0:T(8,128)(2,1)S(1)}, u32[]{:S(2)}, u32[]{:S(2)}) %collective-permute-start) | collective-permute-done | bytes 327712 | tf_op jit(solution)/shard_map/ppermute | solution.py:63
  28.2 1.1 select_bitcast_fusion.1
  29.3 0.9 pad_maximum_fusion
  30.2 0.0 all-gather.3.cloned.1.call-update
  30.2 0.7 collective-permute-start.2
  30.9 1.2 collective-permute-start.5
  32.1 6.8 %collective-permute-start.6 = (bf16[128,1280]{1,0:T(8,128)(2,1)S(1)}, bf16[128,1280]{1,0:T(8,128)(2,1)S(1)}, u32[]{:S(2)}, u32[]{:S(2)}) collective-permute-start(bf16[128,1280]{1,0:T(8,128)(2,1)S(1)} %collective-permute-done), channel_id=1, source_target_pairs={{0,1},{1,0},{2,3},{3,2},{4,5},{5,4},{6,7},{7,6},{8,12},{9,13},{10,... | collective-permute-start | bytes 983048 | tf_op jit(solution)/shard_map/ppermute | solution.py:39
  38.9 1.1 collective-permute-start.4
  40.0 2.5 %collective-permute-done.5 = bf16[128,1280]{1,0:T(8,128)(2,1)S(1)} collective-permute-done((bf16[128,1280]{1,0:T(8,128)(2,1)S(1)}, bf16[128,1280]{1,0:T(8,128)(2,1)S(1)}, u32[]{:S(2)}, u32[]{:S(2)}) %collective-permute-start.5) | collective-permute-done | bytes 327712 | tf_op jit(solution)/shard_map/ppermute | solution.py:39
  42.4 5.1 %collective-permute-done.6 = bf16[128,1280]{1,0:T(8,128)(2,1)S(1)} collective-permute-done((bf16[128,1280]{1,0:T(8,128)(2,1)S(1)}, bf16[128,1280]{1,0:T(8,128)(2,1)S(1)}, u32[]{:S(2)}, u32[]{:S(2)}) %collective-permute-start.6) | collective-permute-done | bytes 327712 | tf_op jit(solution)/shard_map/ppermute | solution.py:39
  47.5 0.1 pad_maximum_fusion.2.refs_1_
  47.6 0.1 collective-permute-start.8
  47.7 0.0 collective-permute-done.4
  47.7 0.1 pad_maximum_fusion.1.refs_0_
  47.8 2.1 %collective-permute-start.7 = (bf16[2,128,1280]{2,1,0:T(8,128)(2,1)S(1)}, bf16[2,128,1280]{2,1,0:T(8,128)(2,1)S(1)}, u32[]{:S(2)}, u32[]{:S(2)}) collective-permute-start(bf16[2,128,1280]{2,1,0:T(8,128)(2,1)S(1)} %pad_maximum_fusion.1.refs_0_), channel_id=1, source_target_pairs={{0,2},{1,3},{2,4},{3,5},{4,6},{5,7},{6,0},{7,1},{8,136},{9,137},{1... | collective-permute-start | bytes 1966088 | tf_op jit(solution)/shard_map/ppermute | solution.py:39
  49.8 0.1 collective-permute-start.10
  49.9 1.9 %collective-permute-start.9 = (bf16[2,128,1280]{2,1,0:T(8,128)(2,1)S(1)}, bf16[2,128,1280]{2,1,0:T(8,128)(2,1)}, u32[]{:S(2)}, u32[]{:S(2)}) collective-permute-start(bf16[2,128,1280]{2,1,0:T(8,128)(2,1)S(1)} %pad_maximum_fusion.1.refs_0_), channel_id=1, source_target_pairs={{0,6},{1,7},{2,0},{3,1},{4,2},{5,3},{6,4},{7,5},{8,137},{9,136},{1... | collective-permute-start | bytes 1966088 | tf_op jit(solution)/shard_map/ppermute | solution.py:39
  51.9 6.4 %collective-permute-done.8.refs_3_ = bf16[2,128,1280]{2,1,0:T(8,128)(2,1)S(1)} collective-permute-done((bf16[2,128,1280]{2,1,0:T(8,128)(2,1)S(1)}, bf16[2,128,1280]{2,1,0:T(8,128)(2,1)S(1)}, u32[]{:S(2)}, u32[]{:S(2)}) %collective-permute-start.8) | collective-permute-done | bytes 655392 | tf_op jit(solution)/shard_map/ppermute | solution.py:39
  58.2 0.0 collective-permute-start.12
  58.2 0.2 collective-permute-done.7.refs_2_
  58.4 2.0 %collective-permute-start.11 = (bf16[2,128,1280]{2,1,0:T(8,128)(2,1)S(1)}, bf16[2,128,1280]{2,1,0:T(8,128)(2,1)}, u32[]{:S(2)}, u32[]{:S(2)}) collective-permute-start(bf16[2,128,1280]{2,1,0:T(8,128)(2,1)S(1)} %collective-permute-done.7.refs_2_), channel_id=1, source_target_pairs={{0,2},{1,3},{2,4},{3,5},{4,6},{5,7},{6,0},{7,1},{8,136},{9,137},{1... | collective-permute-start | bytes 1966088 | tf_op jit(solution)/shard_map/ppermute | solution.py:39
  60.5 0.0 collective-permute-done.2.other_ref
  60.5 0.3 collective-permute-start.3
  60.8 0.7 pad_add_fusion.place_ref
  61.4 6.8 %shard_map.92.x_hbm = bf16[1024,2048]{1,0:T(8,128)(2,1)} custom-call(s32[4]{0:T(128)} %pad_add_fusion.place_ref, bf16[512,4096]{1,0:T(8,128)(2,1)} %bitcast.38, bf16[512,4096]{1,0:T(8,128)(2,1)} %collective-permute-done.2.other_ref), custom_call_target="tpu_custom_call" | custom-call | bytes 12582912 | tf_op jit(solution)/shard_map/pallas_call | solution.py:93
  68.2 0.0 copy-start.7
  68.3 0.0 copy-start.4
  68.3 0.0 collective-permute-done.3.far_mix_ref
  68.3 0.0 collective-permute-done.9.refs_4_
  68.3 4.1 %collective-permute-done.12.refs_7_ = bf16[2,128,1280]{2,1,0:T(8,128)(2,1)} collective-permute-done((bf16[2,128,1280]{2,1,0:T(8,128)(2,1)S(1)}, bf16[2,128,1280]{2,1,0:T(8,128)(2,1)}, u32[]{:S(2)}, u32[]{:S(2)}) %collective-permute-start.12) | collective-permute-done | bytes 655392 | tf_op jit(solution)/shard_map/ppermute | solution.py:39
  72.4 0.2 collective-permute-done.11.refs_6_
  72.6 14.0 %shard_map.93 = (f32[512,512]{1,0:T(8,128)}, f32[512,512]{1,0:T(8,128)}) custom-call(s32[4]{0:T(128)} %pad_add_fusion.place_ref, bf16[1024,2048]{1,0:T(8,128)(2,1)} %shard_map.92.x_hbm, f32[8,512]{1,0:T(8,128)} %bitcast.54, f32[8,512]{1,0:T(8,128)} %copy-done.15, bf16[2,128,1280]{2,1,0:T(8,128)(2,1)} %copy-done.1, bf16[2,128,1280]{2,1,0:T(8,128)(2,1)} %copy-done, ...), custom_call_target="tpu_custom_call" | custom-call | flops 5368709120 | bytes 9437184 | tf_op jit(solution)/shard_map/pallas_call | solution.py:172
  86.6 0.1 collective-permute-start.13
  86.7 2.9 %collective-permute-done.13 = f32[512,512]{1,0:T(8,128)S(1)} collective-permute-done((f32[512,512]{1,0:T(8,128)}, f32[512,512]{1,0:T(8,128)S(1)}, u32[]{:S(2)}, u32[]{:S(2)}) %collective-permute-start.13) | collective-permute-done | bytes 1048608 | tf_op jit(solution)/shard_map/ppermute | solution.py:49
  89.6 1.4 add_convert_fusion.refs_0_
  91.0 0.0 copy-start.2
  91.0 2.5 %collective-permute-start.14 = (bf16[512,512]{1,0:T(8,128)(2,1)S(1)}, bf16[512,512]{1,0:T(8,128)(2,1)S(1)}, u32[]{:S(2)}, u32[]{:S(2)}) collective-permute-start(bf16[512,512]{1,0:T(8,128)(2,1)S(1)} %add_convert_fusion.refs_0_), channel_id=1, source_target_pairs={{0,1},{1,0},{2,3},{3,2},{4,5},{5,4},{6,7},{7,6},{8,9},{9,8},{10,11... | collective-permute-start | bytes 1572872 | tf_op jit(solution)/shard_map/ppermute | solution.py:432
  93.5 1.3 collective-permute-start.16
  94.8 3.4 %collective-permute-start.15 = (bf16[512,512]{1,0:T(8,128)(2,1)S(1)}, bf16[512,512]{1,0:T(8,128)(2,1)S(1)}, u32[]{:S(2)}, u32[]{:S(2)}) collective-permute-start(bf16[512,512]{1,0:T(8,128)(2,1)S(1)} %add_convert_fusion.refs_0_), channel_id=1, source_target_pairs={{0,2},{2,4},{4,6},{1,3},{3,5},{5,7},{8,10},{10,12},{12,14},{9,11},... | collective-permute-start | bytes 1572872 | tf_op jit(solution)/shard_map/ppermute | solution.py:433
  98.2 1.5 collective-permute-start.17
  99.7 6.9 %collective-permute-done.14.refs_1_ = bf16[512,512]{1,0:T(8,128)(2,1)S(1)} collective-permute-done((bf16[512,512]{1,0:T(8,128)(2,1)S(1)}, bf16[512,512]{1,0:T(8,128)(2,1)S(1)}, u32[]{:S(2)}, u32[]{:S(2)}) %collective-permute-start.14) | collective-permute-done | bytes 524320 | tf_op jit(solution)/shard_map/ppermute | solution.py:432
  106.5 3.9 %collective-permute-start.18 = (bf16[512,512]{1,0:T(8,128)(2,1)S(1)}, bf16[512,512]{1,0:T(8,128)(2,1)S(1)}, u32[]{:S(2)}, u32[]{:S(2)}) collective-permute-start(bf16[512,512]{1,0:T(8,128)(2,1)S(1)} %collective-permute-done.14.refs_1_), channel_id=1, source_target_pairs={{0,2},{2,4},{4,6},{1,3},{3,5},{5,7},{8,10},{10,12},{12,14},{9,11},... | collective-permute-start | bytes 1572872 | tf_op jit(solution)/shard_map/ppermute | solution.py:436
  110.4 0.7 collective-permute-start.20
  111.1 0.6 collective-permute-done.16.refs_3_
  111.7 1.5 collective-permute-start.19
  113.2 0.6 reshape.42
  113.8 5.1 %shard_map.91.q_ref = bf16[512,256]{1,0:T(8,128)(2,1)} custom-call(bf16[512,4096]{1,0:T(8,128)(2,1)} %bitcast.39, bf16[16,2,1280,128]{3,2,1,0:T(8,128)(2,1)} %bitcast.40), custom_call_target="tpu_custom_call" | custom-call | flops 1073741824 | bytes 6291456 | tf_op jit(solution)/shard_map/pallas_call | solution.py:222
  118.9 2.9 %collective-permute-done.15.refs_2_ = bf16[512,512]{1,0:T(8,128)(2,1)S(1)} collective-permute-done((bf16[512,512]{1,0:T(8,128)(2,1)S(1)}, bf16[512,512]{1,0:T(8,128)(2,1)S(1)}, u32[]{:S(2)}, u32[]{:S(2)}) %collective-permute-start.15) | collective-permute-done | bytes 524320 | tf_op jit(solution)/shard_map/ppermute | solution.py:433
  121.9 0.0 collective-permute-done.17.refs_4_
  121.9 0.8 copy-done.14
  122.6 7.3 %shard_map.94 = (f32[2,512]{1,0:T(2,128)}, f32[2,512]{1,0:T(2,128)}, f32[256,512]{1,0:T(8,128)}) custom-call(s32[4]{0:T(128)} %pad_add_fusion.place_ref, bf16[512,256]{1,0:T(8,128)(2,1)} %shard_map.91.q_ref, bf16[512,512]{1,0:T(8,128)(2,1)} %copy-done.2, bf16[512,512]{1,0:T(8,128)(2,1)} %copy-done.10, bf16[512,512]{1,0:T(8,128)(2,1)} %copy-done.14, ...), custom_call_target="tpu_custom_call" | custom-call | flops 1342177280 | bytes 2621440 | tf_op jit(solution)/shard_map/pallas_call | solution.py:362
  130.0 3.0 %collective-permute-done.18.refs_0_ = bf16[512,512]{1,0:T(8,128)(2,1)S(1)} collective-permute-done((bf16[512,512]{1,0:T(8,128)(2,1)S(1)}, bf16[512,512]{1,0:T(8,128)(2,1)S(1)}, u32[]{:S(2)}, u32[]{:S(2)}) %collective-permute-start.18) | collective-permute-done | bytes 524320 | tf_op jit(solution)/shard_map/ppermute | solution.py:436
  133.0 0.0 collective-permute-done.19.refs_1_
  133.0 0.0 collective-permute-done.20.refs_2_
  133.0 0.8 copy-done.12
  133.8 0.2 copy-done.13
  134.0 10.3 %shard_map.95 = bf16[512,4096]{1,0:T(8,128)(2,1)} custom-call(s32[4]{0:T(128)} %pad_add_fusion.place_ref, bf16[512,256]{1,0:T(8,128)(2,1)} %shard_map.91.q_ref, f32[2,512]{1,0:T(2,128)} %get-tuple-element.16.m_in, f32[2,512]{1,0:T(2,128)} %get-tuple-element.17.l_in, f32[256,512]{1,0:T(8,128)} %get-tuple-element.18.acc_in, f32[8,512]{1,0:T(8,128)} %bitcast.52, ...), custom_call_target="tpu_custom_call" | custom-call | flops 5100273664 | bytes 1572864 | tf_op jit(solution)/shard_map/pallas_call | solution.py:379
  (35 shorter events, 0.1 us)
Async XLA Ops:
  6.5 53.9 %copy-start.6 = (bf16[1,512,2,2]{1,3,2,0:T(2,128)(2,1)S(1)}, bf16[1,512,2,2]{1,3,2,0:T(2,128)(2,1)}, u32[]{:S(2)}) copy-start(bf16[1,512,2,2]{1,3,2,0:T(2,128)(2,1)} %param.15) | copy-start | bytes 12292
  6.5 53.9 %copy-start.5 = (s32[1,512,2,2]{1,3,2,0:T(2,128)S(1)}, s32[1,512,2,2]{1,3,2,0:T(2,128)}, u32[]{:S(2)}) copy-start(s32[1,512,2,2]{1,3,2,0:T(2,128)} %param.14) | copy-start | bytes 24580
  6.5 107.3 %all-gather.3.cloned.1.call-start = ((), (), s32[]{:S(2)}) async-start(), calls=%async_computation | async-start | bytes 11141120 | tf_op jit(solution)/shard_map/all_gather | solution.py:427
  8.4 10.7 %collective-permute-start.1 = (bf16[1280,128]{1,0:T(8,128)(2,1)S(1)}, bf16[1280,128]{1,0:T(8,128)(2,1)S(1)}, u32[]{:S(2)}, u32[]{:S(2)}) collective-permute-start(bf16[1280,128]{1,0:T(8,128)(2,1)S(1)} %pad_maximum_fusion.3), channel_id=1, source_target_pairs={{0,128},{128,0},{1,129},{129,1},{2,130},{130,2},{3,131},{131,3},{4... | collective-permute-start | bytes 983048 | tf_op jit(solution)/shard_map/ppermute | solution.py:421
  11.3 16.9 %collective-permute-start = (bf16[128,1280]{1,0:T(8,128)(2,1)S(1)}, bf16[128,1280]{1,0:T(8,128)(2,1)S(1)}, u32[]{:S(2)}, u32[]{:S(2)}) collective-permute-start(bf16[128,1280]{1,0:T(8,128)(2,1)S(1)} %pad_maximum_fusion.4), channel_id=1, source_target_pairs={{0,0},{1,17},{2,34},{3,51},{4,68},{5,85},{6,102},{7,119},{8,8},{9,... | collective-permute-start | bytes 983048 | tf_op jit(solution)/shard_map/ppermute | solution.py:63
  30.2 30.2 %collective-permute-start.2 = (bf16[512,4096]{1,0:T(8,128)(2,1)}, bf16[512,4096]{1,0:T(8,128)(2,1)}, u32[]{:S(2)}, u32[]{:S(2)}) collective-permute-start(bf16[512,4096]{1,0:T(8,128)(2,1)} %bitcast.37), channel_id=1, source_target_pairs={{0,8},{8,0},{1,9},{9,1},{2,10},{10,2},{3,11},{11,3},{4,12},{12,4},... | collective-permute-start | bytes 12582920 | tf_op jit(solution)/shard_map/ppermute | solution.py:49
  30.9 11.6 %collective-permute-start.5 = (bf16[128,1280]{1,0:T(8,128)(2,1)S(1)}, bf16[128,1280]{1,0:T(8,128)(2,1)S(1)}, u32[]{:S(2)}, u32[]{:S(2)}) collective-permute-start(bf16[128,1280]{1,0:T(8,128)(2,1)S(1)} %collective-permute-done), channel_id=1, source_target_pairs={{0,129},{1,128},{2,131},{3,130},{4,133},{5,132},{6,135},{7,134},{8... | collective-permute-start | bytes 983048 | tf_op jit(solution)/shard_map/ppermute | solution.py:39
  32.1 15.4 %collective-permute-start.6 = (bf16[128,1280]{1,0:T(8,128)(2,1)S(1)}, bf16[128,1280]{1,0:T(8,128)(2,1)S(1)}, u32[]{:S(2)}, u32[]{:S(2)}) collective-permute-start(bf16[128,1280]{1,0:T(8,128)(2,1)S(1)} %collective-permute-done), channel_id=1, source_target_pairs={{0,1},{1,0},{2,3},{3,2},{4,5},{5,4},{6,7},{7,6},{8,12},{9,13},{10,... | collective-permute-start | bytes 983048 | tf_op jit(solution)/shard_map/ppermute | solution.py:39
  38.9 8.8 %collective-permute-start.4 = (bf16[128,1280]{1,0:T(8,128)(2,1)S(1)}, bf16[128,1280]{1,0:T(8,128)(2,1)S(1)}, u32[]{:S(2)}, u32[]{:S(2)}) collective-permute-start(bf16[128,1280]{1,0:T(8,128)(2,1)S(1)} %collective-permute-done), channel_id=1, source_target_pairs={{0,128},{1,129},{2,130},{3,131},{4,132},{5,133},{6,134},{7,135},{8... | collective-permute-start | bytes 983048 | tf_op jit(solution)/shard_map/ppermute | solution.py:39
  47.6 20.7 %copy-start = (bf16[2,128,1280]{2,1,0:T(8,128)(2,1)}, bf16[2,128,1280]{2,1,0:T(8,128)(2,1)S(1)}, u32[]{:S(2)}) copy-start(bf16[2,128,1280]{2,1,0:T(8,128)(2,1)S(1)} %pad_maximum_fusion.2.refs_1_) | copy-start | bytes 1966084
  47.6 10.7 %collective-permute-start.8 = (bf16[2,128,1280]{2,1,0:T(8,128)(2,1)S(1)}, bf16[2,128,1280]{2,1,0:T(8,128)(2,1)S(1)}, u32[]{:S(2)}, u32[]{:S(2)}) collective-permute-start(bf16[2,128,1280]{2,1,0:T(8,128)(2,1)S(1)} %pad_maximum_fusion.2.refs_1_), channel_id=1, source_target_pairs={{0,6},{1,7},{2,0},{3,1},{4,2},{5,3},{6,4},{7,5},{8,137},{9,136},{1... | collective-permute-start | bytes 1966088 | tf_op jit(solution)/shard_map/ppermute | solution.py:39
  47.7 20.5 %copy-start.1 = (bf16[2,128,1280]{2,1,0:T(8,128)(2,1)}, bf16[2,128,1280]{2,1,0:T(8,128)(2,1)S(1)}, u32[]{:S(2)}) copy-start(bf16[2,128,1280]{2,1,0:T(8,128)(2,1)S(1)} %pad_maximum_fusion.1.refs_0_) | copy-start | bytes 1966084
  47.8 10.7 %collective-permute-start.7 = (bf16[2,128,1280]{2,1,0:T(8,128)(2,1)S(1)}, bf16[2,128,1280]{2,1,0:T(8,128)(2,1)S(1)}, u32[]{:S(2)}, u32[]{:S(2)}) collective-permute-start(bf16[2,128,1280]{2,1,0:T(8,128)(2,1)S(1)} %pad_maximum_fusion.1.refs_0_), channel_id=1, source_target_pairs={{0,2},{1,3},{2,4},{3,5},{4,6},{5,7},{6,0},{7,1},{8,136},{9,137},{1... | collective-permute-start | bytes 1966088 | tf_op jit(solution)/shard_map/ppermute | solution.py:39
  49.8 18.5 %collective-permute-start.10 = (bf16[2,128,1280]{2,1,0:T(8,128)(2,1)S(1)}, bf16[2,128,1280]{2,1,0:T(8,128)(2,1)}, u32[]{:S(2)}, u32[]{:S(2)}) collective-permute-start(bf16[2,128,1280]{2,1,0:T(8,128)(2,1)S(1)} %pad_maximum_fusion.2.refs_1_), channel_id=1, source_target_pairs={{0,2},{1,3},{2,4},{3,5},{4,6},{5,7},{6,0},{7,1},{8,136},{9,137},{1... | collective-permute-start | bytes 1966088 | tf_op jit(solution)/shard_map/ppermute | solution.py:39
  49.9 18.4 %collective-permute-start.9 = (bf16[2,128,1280]{2,1,0:T(8,128)(2,1)S(1)}, bf16[2,128,1280]{2,1,0:T(8,128)(2,1)}, u32[]{:S(2)}, u32[]{:S(2)}) collective-permute-start(bf16[2,128,1280]{2,1,0:T(8,128)(2,1)S(1)} %pad_maximum_fusion.1.refs_0_), channel_id=1, source_target_pairs={{0,6},{1,7},{2,0},{3,1},{4,2},{5,3},{6,4},{7,5},{8,137},{9,136},{1... | collective-permute-start | bytes 1966088 | tf_op jit(solution)/shard_map/ppermute | solution.py:39
  58.2 10.0 %copy-start.8 = (bf16[2,128,1280]{2,1,0:T(8,128)(2,1)}, bf16[2,128,1280]{2,1,0:T(8,128)(2,1)S(1)}, u32[]{:S(2)}) copy-start(bf16[2,128,1280]{2,1,0:T(8,128)(2,1)S(1)} %collective-permute-done.8.refs_3_) | copy-start | bytes 1966084
  58.2 14.1 %collective-permute-start.12 = (bf16[2,128,1280]{2,1,0:T(8,128)(2,1)S(1)}, bf16[2,128,1280]{2,1,0:T(8,128)(2,1)}, u32[]{:S(2)}, u32[]{:S(2)}) collective-permute-start(bf16[2,128,1280]{2,1,0:T(8,128)(2,1)S(1)} %collective-permute-done.8.refs_3_), channel_id=1, source_target_pairs={{0,6},{1,7},{2,0},{3,1},{4,2},{5,3},{6,4},{7,5},{8,137},{9,136},{1... | collective-permute-start | bytes 1966088 | tf_op jit(solution)/shard_map/ppermute | solution.py:39
  58.4 9.8 %copy-start.9 = (bf16[2,128,1280]{2,1,0:T(8,128)(2,1)}, bf16[2,128,1280]{2,1,0:T(8,128)(2,1)S(1)}, u32[]{:S(2)}) copy-start(bf16[2,128,1280]{2,1,0:T(8,128)(2,1)S(1)} %collective-permute-done.7.refs_2_) | copy-start | bytes 1966084
  58.4 14.1 %collective-permute-start.11 = (bf16[2,128,1280]{2,1,0:T(8,128)(2,1)S(1)}, bf16[2,128,1280]{2,1,0:T(8,128)(2,1)}, u32[]{:S(2)}, u32[]{:S(2)}) collective-permute-start(bf16[2,128,1280]{2,1,0:T(8,128)(2,1)S(1)} %collective-permute-done.7.refs_2_), channel_id=1, source_target_pairs={{0,2},{1,3},{2,4},{3,5},{4,6},{5,7},{6,0},{7,1},{8,136},{9,137},{1... | collective-permute-start | bytes 1966088 | tf_op jit(solution)/shard_map/ppermute | solution.py:39
  60.5 7.8 %copy-start.3 = (f32[512,8]{0,1:T(8,128)}, f32[512,8]{0,1:T(8,128)S(1)}, u32[]{:S(2)}) copy-start(f32[512,8]{0,1:T(8,128)S(1)} %reshape.39) | copy-start | bytes 49156
  60.5 7.8 %collective-permute-start.3 = (f32[8,512]{1,0:T(8,128)S(1)}, f32[8,512]{1,0:T(8,128)S(1)}, u32[]{:S(2)}, u32[]{:S(2)}) collective-permute-start(f32[8,512]{1,0:T(8,128)S(1)} %bitcast.53), channel_id=1, source_target_pairs={{0,8},{8,0},{1,9},{9,1},{2,10},{10,2},{3,11},{11,3},{4,12},{12,4},... | collective-permute-start | bytes 49160 | tf_op jit(solution)/shard_map/ppermute | solution.py:49
  68.2 44.9 %copy-start.7 = (bf16[1,512,2,2]{1,3,2,0:T(2,128)(2,1)S(1)}, bf16[1,512,2,2]{1,3,2,0:T(2,128)(2,1)}, u32[]{:S(2)}) copy-start(bf16[1,512,2,2]{1,3,2,0:T(2,128)(2,1)} %param.17) | copy-start | bytes 12292
  68.3 44.9 %copy-start.4 = (s32[1,512,2,2]{1,3,2,0:T(2,128)S(1)}, s32[1,512,2,2]{1,3,2,0:T(2,128)}, u32[]{:S(2)}) copy-start(s32[1,512,2,2]{1,3,2,0:T(2,128)} %param.16) | copy-start | bytes 24580
  68.3 4.3 %copy-start.15 = (f32[8,512]{1,0:T(8,128)}, f32[8,512]{1,0:T(8,128)S(1)}, u32[]{:S(2)}) copy-start(f32[8,512]{1,0:T(8,128)S(1)} %collective-permute-done.3.far_mix_ref) | copy-start | bytes 49156
  86.6 3.0 %collective-permute-start.13 = (f32[512,512]{1,0:T(8,128)}, f32[512,512]{1,0:T(8,128)S(1)}, u32[]{:S(2)}, u32[]{:S(2)}) collective-permute-start(f32[512,512]{1,0:T(8,128)} %get-tuple-element.15), channel_id=1, source_target_pairs={{0,8},{8,0},{1,9},{9,1},{2,10},{10,2},{3,11},{11,3},{4,12},{12,4},... | collective-permute-start | bytes 3145736 | tf_op jit(solution)/shard_map/ppermute | solution.py:49
  91.0 27.9 %copy-start.2 = (bf16[512,512]{1,0:T(8,128)(2,1)}, bf16[512,512]{1,0:T(8,128)(2,1)S(1)}, u32[]{:S(2)}) copy-start(bf16[512,512]{1,0:T(8,128)(2,1)S(1)} %add_convert_fusion.refs_0_) | copy-start | bytes 1572868
  91.0 15.5 %collective-permute-start.14 = (bf16[512,512]{1,0:T(8,128)(2,1)S(1)}, bf16[512,512]{1,0:T(8,128)(2,1)S(1)}, u32[]{:S(2)}, u32[]{:S(2)}) collective-permute-start(bf16[512,512]{1,0:T(8,128)(2,1)S(1)} %add_convert_fusion.refs_0_), channel_id=1, source_target_pairs={{0,1},{1,0},{2,3},{3,2},{4,5},{5,4},{6,7},{7,6},{8,9},{9,8},{10,11... | collective-permute-start | bytes 1572872 | tf_op jit(solution)/shard_map/ppermute | solution.py:432
  93.5 18.2 %collective-permute-start.16 = (bf16[512,512]{1,0:T(8,128)(2,1)S(1)}, bf16[512,512]{1,0:T(8,128)(2,1)S(1)}, u32[]{:S(2)}, u32[]{:S(2)}) collective-permute-start(bf16[512,512]{1,0:T(8,128)(2,1)S(1)} %add_convert_fusion.refs_0_), channel_id=1, source_target_pairs={{0,4},{2,6},{1,5},{3,7},{8,12},{10,14},{9,13},{11,15},{16,20},{18,... | collective-permute-start | bytes 1572872 | tf_op jit(solution)/shard_map/ppermute | solution.py:435
  94.8 27.1 %collective-permute-start.15 = (bf16[512,512]{1,0:T(8,128)(2,1)S(1)}, bf16[512,512]{1,0:T(8,128)(2,1)S(1)}, u32[]{:S(2)}, u32[]{:S(2)}) collective-permute-start(bf16[512,512]{1,0:T(8,128)(2,1)S(1)} %add_convert_fusion.refs_0_), channel_id=1, source_target_pairs={{0,2},{2,4},{4,6},{1,3},{3,5},{5,7},{8,10},{10,12},{12,14},{9,11},... | collective-permute-start | bytes 1572872 | tf_op jit(solution)/shard_map/ppermute | solution.py:433
  98.2 23.7 %collective-permute-start.17 = (bf16[512,512]{1,0:T(8,128)(2,1)S(1)}, bf16[512,512]{1,0:T(8,128)(2,1)}, u32[]{:S(2)}, u32[]{:S(2)}) collective-permute-start(bf16[512,512]{1,0:T(8,128)(2,1)S(1)} %add_convert_fusion.refs_0_), channel_id=1, source_target_pairs={{0,6},{1,7},{8,14},{9,15},{16,22},{17,23},{24,30},{25,31},{32,38},... | collective-permute-start | bytes 1572872 | tf_op jit(solution)/shard_map/ppermute | solution.py:434
  106.5 12.4 %copy-start.10 = (bf16[512,512]{1,0:T(8,128)(2,1)}, bf16[512,512]{1,0:T(8,128)(2,1)S(1)}, u32[]{:S(2)}) copy-start(bf16[512,512]{1,0:T(8,128)(2,1)S(1)} %collective-permute-done.14.refs_1_) | copy-start | bytes 1572868
  106.5 26.5 %collective-permute-start.18 = (bf16[512,512]{1,0:T(8,128)(2,1)S(1)}, bf16[512,512]{1,0:T(8,128)(2,1)S(1)}, u32[]{:S(2)}, u32[]{:S(2)}) collective-permute-start(bf16[512,512]{1,0:T(8,128)(2,1)S(1)} %collective-permute-done.14.refs_1_), channel_id=1, source_target_pairs={{0,2},{2,4},{4,6},{1,3},{3,5},{5,7},{8,10},{10,12},{12,14},{9,11},... | collective-permute-start | bytes 1572872 | tf_op jit(solution)/shard_map/ppermute | solution.py:436
  110.4 22.6 %collective-permute-start.20 = (bf16[512,512]{1,0:T(8,128)(2,1)S(1)}, bf16[512,512]{1,0:T(8,128)(2,1)S(1)}, u32[]{:S(2)}, u32[]{:S(2)}) collective-permute-start(bf16[512,512]{1,0:T(8,128)(2,1)S(1)} %collective-permute-done.14.refs_1_), channel_id=1, source_target_pairs={{0,6},{1,7},{8,14},{9,15},{16,22},{17,23},{24,30},{25,31},{32,38},... | collective-permute-start | bytes 1572872 | tf_op jit(solution)/shard_map/ppermute | solution.py:437
  111.7 7.2 %copy-start.11 = (bf16[512,512]{1,0:T(8,128)(2,1)}, bf16[512,512]{1,0:T(8,128)(2,1)S(1)}, u32[]{:S(2)}) copy-start(bf16[512,512]{1,0:T(8,128)(2,1)S(1)} %collective-permute-done.16.refs_3_) | copy-start | bytes 1572868
  111.7 21.3 %collective-permute-start.19 = (bf16[512,512]{1,0:T(8,128)(2,1)S(1)}, bf16[512,512]{1,0:T(8,128)(2,1)}, u32[]{:S(2)}, u32[]{:S(2)}) collective-permute-start(bf16[512,512]{1,0:T(8,128)(2,1)S(1)} %collective-permute-done.16.refs_3_), channel_id=1, source_target_pairs={{0,1},{1,0},{2,3},{3,2},{4,5},{5,4},{6,7},{7,6},{8,9},{9,8},{10,11... | collective-permute-start | bytes 1572872 | tf_op jit(solution)/shard_map/ppermute | solution.py:438
  121.9 0.8 copy-start.14
  133.0 0.8 copy-start.12
  133.0 1.0 copy-start.13
Sparse Core Ops, SparseCore 0:
  30.4 69.1 all-gather.2
where the time goes:
time: 153 us; the launch traced here: 151 us
  waiting for transfers between devices  43.7 us (29%)
  Pallas kernels  43.6 us (28%)
  starting transfers between devices  39.7 us (26%)
  between operations  13.7 us (9%)
  local copies, waits for them, and re-layouts  5.3 us (3%)
  other arithmetic  5.24 us (3%)
    ppermute x9, waiting for transfers between devices, moved(): return lax.ppermute(x, AXES, pairs)  18.3 us
    ppermute x9, starting transfers between devices, moved(): return lax.ppermute(x, AXES, pairs)  15.3 us
    pallas_call x1, Pallas kernels, project(): pl.pallas_call(functools.partial(project_kernel, count), in_specs=[pl.Blo...  14 us
    pallas_call x1, Pallas kernels, attend_late(): pl.pallas_call(functools.partial(attend_late_kernel, needs), in_specs=[pl...  10.3 us
    ppermute x1, waiting for transfers between devices, lifted(): return lax.ppermute(x, AXES, pairs)  9.13 us
    ppermute x1, starting transfers between devices, lifted(): return lax.ppermute(x, AXES, pairs)  7.75 us
    pallas_call x1, Pallas kernels, attend_early(): pl.pallas_call(functools.partial(attend_early_kernel, needs), in_specs=[p...  7.34 us
    ppermute x1, waiting for transfers between devices, on_device(): other = lax.ppermute(own, 'x_hi', [(0, 1), (1, 0)])  6.86 us
  transfers between devices with their start and end apart: 22, of which 12 were waited for; matrix products, arithmetic and copies ran while one was open for 3% of the time, Pallas kernels for 22%

commit v1 on v0

--- a/solution.py
+++ b/solution.py
@@ -26,7 +26,7 @@
 
 
 RING = 4
-VM = pltpu.CompilerParams(vmem_limit_bytes=60 * MIB)
+VM = pltpu.CompilerParams(vmem_limit_bytes=32 * MIB)
 
 
 def moved(x, target):

time: 153 us -> 147 us (0.961)
  Pallas kernels: 43.6 us -> 32.4 us
  local copies, waits for them, and re-layouts: 5.3 us -> 11.3 us
  other arithmetic: 5.24 us -> 3.49 us
    unnamed x34 -> x18, local copies, waits for them, and re-layouts: 3.56 us -> 10.2 us
    pallas_call x1, Pallas kernels: 14 us -> 9.98 us  [project(): pl.pallas_call(functools.partial(project_kernel, count), in_specs=[pl.Blo...]
    pallas_call x1, Pallas kernels: 6.78 us -> 3.44 us  [packed(): pl.pallas_call(pack_kernel, in_specs=[pl.BlockSpec(memory_space=pltpu.SME...]
    ppermute x1, waiting for transfers between devices: 2.94 us -> 0.05 us  [on_device(): own_1 = lax.ppermute(own, 'y', [(0, 1), (1, 2), (2, 3)])]
    pallas_call x1, Pallas kernels: 5.07 us -> 2.52 us  [query(): pl.pallas_call(query_kernel, grid=(steps,), in_specs=[pl.BlockSpec((rows,...]
    ppermute x1, waiting for transfers between devices: 3.02 us -> 4.83 us  [on_device(): other_1 = lax.ppermute(other, 'y', [(0, 1), (1, 2), (2, 3)])]
    ppermute x9, waiting for transfers between devices: 18.3 us -> 20 us  [moved(): return lax.ppermute(x, AXES, pairs)]
  transfers between devices with their start and end apart: 22 -> 22, of which waited for: 12 -> 11; matrix products, arithmetic and copies ran while one was open for 3% -> 2% of each run, Pallas kernels for 22% -> 15%
where the time goes in v1:
time: 147 us; the launch traced here: 145 us
  waiting for transfers between devices  44.4 us (30%)
  starting transfers between devices  39.4 us (27%)
  Pallas kernels  32.4 us (22%)
  between operations  13.7 us (9%)
  local copies, waits for them, and re-layouts  11.3 us (8%)
  other arithmetic  3.49 us (2%)
    ppermute x9, waiting for transfers between devices, moved(): return lax.ppermute(x, AXES, pairs)  20 us
    ppermute x9, starting transfers between devices, moved(): return lax.ppermute(x, AXES, pairs)  15.3 us
    pallas_call x1, Pallas kernels, attend_late(): pl.pallas_call(functools.partial(attend_late_kernel, needs), in_specs=[pl...  10.2 us
    unnamed x18, local copies, waits for them, and re-layouts  10.2 us
    pallas_call x1, Pallas kernels, project(): pl.pallas_call(functools.partial(project_kernel, count), in_specs=[pl.Blo...  9.98 us
    ppermute x1, waiting for transfers between devices, lifted(): return lax.ppermute(x, AXES, pairs)  9.13 us
    ppermute x1, starting transfers between devices, lifted(): return lax.ppermute(x, AXES, pairs)  7.75 us
    ppermute x1, waiting for transfers between devices, on_device(): other = lax.ppermute(own, 'x_hi', [(0, 1), (1, 0)])  6.99 us
  transfers between devices with their start and end apart: 22, of which 11 were waited for; matrix products, arithmetic and copies ran while one was open for 2% of the time, Pallas kernels for 15%

profile of v1, /device:TPU:54, one launch (start us, length us, event | category | flops | bytes accessed | tf_op | source)
XLA Modules:
  0.0 144.7 jit_solution(3612978616881182161)
XLA Ops:
  6.5 0.9 copy.24
  7.4 1.0 pad_maximum_fusion.3
  8.4 0.9 collective-permute-start.1
  9.3 1.1 reshape.38
  10.4 0.9 copy.27
  11.3 7.8 %collective-permute-start = (bf16[128,1280]{1,0:T(8,128)(2,1)S(1)}, bf16[128,1280]{1,0:T(8,128)(2,1)S(1)}, u32[]{:S(2)}, u32[]{:S(2)}) collective-permute-start(bf16[128,1280]{1,0:T(8,128)(2,1)S(1)} %pad_maximum_fusion.4), channel_id=1, source_target_pairs={{0,0},{1,17},{2,34},{3,51},{4,68},{5,85},{6,102},{7,119},{8,8},{9,... | collective-permute-start | bytes 983048 | tf_op jit(solution)/shard_map/ppermute | solution.py:63
  19.1 0.0 collective-permute-done.1
  19.1 9.1 %collective-permute-done = bf16[128,1280]{1,0:T(8,128)(2,1)S(1)} collective-permute-done((bf16[128,1280]{1,0:T(8,128)(2,1)S(1)}, bf16[128,1280]{1,0:T(8,128)(2,1)S(1)}, u32[]{:S(2)}, u32[]{:S(2)}) %collective-permute-start) | collective-permute-done | bytes 327712 | tf_op jit(solution)/shard_map/ppermute | solution.py:63
  28.2 1.1 select_bitcast_fusion.1
  29.3 0.9 pad_maximum_fusion
  30.2 0.0 all-gather.3.cloned.1.call-update
  30.2 0.7 collective-permute-start.2
  30.9 1.2 collective-permute-start.5
  32.1 6.8 %collective-permute-start.6 = (bf16[128,1280]{1,0:T(8,128)(2,1)S(1)}, bf16[128,1280]{1,0:T(8,128)(2,1)S(1)}, u32[]{:S(2)}, u32[]{:S(2)}) collective-permute-start(bf16[128,1280]{1,0:T(8,128)(2,1)S(1)} %collective-permute-done), channel_id=1, source_target_pairs={{0,1},{1,0},{2,3},{3,2},{4,5},{5,4},{6,7},{7,6},{8,12},{9,13},{10,... | collective-permute-start | bytes 983048 | tf_op jit(solution)/shard_map/ppermute | solution.py:39
  38.8 1.1 collective-permute-start.4
  40.0 2.5 %collective-permute-done.5 = bf16[128,1280]{1,0:T(8,128)(2,1)S(1)} collective-permute-done((bf16[128,1280]{1,0:T(8,128)(2,1)S(1)}, bf16[128,1280]{1,0:T(8,128)(2,1)S(1)}, u32[]{:S(2)}, u32[]{:S(2)}) %collective-permute-start.5) | collective-permute-done | bytes 327712 | tf_op jit(solution)/shard_map/ppermute | solution.py:39
  42.4 5.1 %collective-permute-done.6 = bf16[128,1280]{1,0:T(8,128)(2,1)S(1)} collective-permute-done((bf16[128,1280]{1,0:T(8,128)(2,1)S(1)}, bf16[128,1280]{1,0:T(8,128)(2,1)S(1)}, u32[]{:S(2)}, u32[]{:S(2)}) %collective-permute-start.6) | collective-permute-done | bytes 327712 | tf_op jit(solution)/shard_map/ppermute | solution.py:39
  47.5 0.1 pad_maximum_fusion.2.refs_1_
  47.5 0.1 collective-permute-start.8
  47.6 0.0 collective-permute-done.4
  47.7 0.1 pad_maximum_fusion.1.refs_0_
  47.7 2.1 %collective-permute-start.7 = (bf16[2,128,1280]{2,1,0:T(8,128)(2,1)S(1)}, bf16[2,128,1280]{2,1,0:T(8,128)(2,1)S(1)}, u32[]{:S(2)}, u32[]{:S(2)}) collective-permute-start(bf16[2,128,1280]{2,1,0:T(8,128)(2,1)S(1)} %pad_maximum_fusion.1.refs_0_), channel_id=1, source_target_pairs={{0,2},{1,3},{2,4},{3,5},{4,6},{5,7},{6,0},{7,1},{8,136},{9,137},{1... | collective-permute-start | bytes 1966088 | tf_op jit(solution)/shard_map/ppermute | solution.py:39
  49.8 0.1 collective-permute-start.10
  49.9 1.9 %collective-permute-start.9 = (bf16[2,128,1280]{2,1,0:T(8,128)(2,1)S(1)}, bf16[2,128,1280]{2,1,0:T(8,128)(2,1)}, u32[]{:S(2)}, u32[]{:S(2)}) collective-permute-start(bf16[2,128,1280]{2,1,0:T(8,128)(2,1)S(1)} %pad_maximum_fusion.1.refs_0_), channel_id=1, source_target_pairs={{0,6},{1,7},{2,0},{3,1},{4,2},{5,3},{6,4},{7,5},{8,137},{9,136},{1... | collective-permute-start | bytes 1966088 | tf_op jit(solution)/shard_map/ppermute | solution.py:39
  51.8 6.4 %collective-permute-done.8.refs_3_ = bf16[2,128,1280]{2,1,0:T(8,128)(2,1)S(1)} collective-permute-done((bf16[2,128,1280]{2,1,0:T(8,128)(2,1)S(1)}, bf16[2,128,1280]{2,1,0:T(8,128)(2,1)S(1)}, u32[]{:S(2)}, u32[]{:S(2)}) %collective-permute-start.8) | collective-permute-done | bytes 655392 | tf_op jit(solution)/shard_map/ppermute | solution.py:39
  58.2 0.0 collective-permute-start.12
  58.2 0.2 collective-permute-done.7.refs_2_
  58.4 2.0 %collective-permute-start.11 = (bf16[2,128,1280]{2,1,0:T(8,128)(2,1)S(1)}, bf16[2,128,1280]{2,1,0:T(8,128)(2,1)}, u32[]{:S(2)}, u32[]{:S(2)}) collective-permute-start(bf16[2,128,1280]{2,1,0:T(8,128)(2,1)S(1)} %collective-permute-done.7.refs_2_), channel_id=1, source_target_pairs={{0,2},{1,3},{2,4},{3,5},{4,6},{5,7},{6,0},{7,1},{8,136},{9,137},{1... | collective-permute-start | bytes 1966088 | tf_op jit(solution)/shard_map/ppermute | solution.py:39
  60.4 0.0 collective-permute-done.2.other_ref
  60.5 0.3 collective-permute-start.3
  60.7 0.1 pad_add_fusion.place_ref
  60.8 2.3 %copy-done = bf16[1,512,4096]{2,1,0:T(8,128)(2,1)S(1)} copy-done((bf16[1,512,4096]{2,1,0:T(8,128)(2,1)S(1)}, bf16[1,512,4096]{2,1,0:T(8,128)(2,1)}, u32[]{:S(2)}) %copy-start) | copy-done | bytes 4194328
  63.1 3.4 %shard_map.92.x_hbm = bf16[1024,2048]{1,0:T(8,128)(2,1)S(1)} custom-call(s32[4]{0:T(128)S(1)} %pad_add_fusion.place_ref, bf16[512,4096]{1,0:T(8,128)(2,1)S(1)} %bitcast.38, bf16[512,4096]{1,0:T(8,128)(2,1)} %collective-permute-done.2.other_ref), custom_call_target="tpu_custom_call" | custom-call | bytes 12582912 | tf_op jit(solution)/shard_map/pallas_call | solution.py:93
  66.5 0.0 copy-start.7
  66.5 0.0 copy-start.4
  66.5 0.0 collective-permute-done.10.refs_5_
  66.6 0.0 collective-permute-done.9.refs_4_
  66.6 5.8 %collective-permute-done.12.refs_7_ = bf16[2,128,1280]{2,1,0:T(8,128)(2,1)} collective-permute-done((bf16[2,128,1280]{2,1,0:T(8,128)(2,1)S(1)}, bf16[2,128,1280]{2,1,0:T(8,128)(2,1)}, u32[]{:S(2)}, u32[]{:S(2)}) %collective-permute-start.12) | collective-permute-done | bytes 655392 | tf_op jit(solution)/shard_map/ppermute | solution.py:39
  72.4 0.2 collective-permute-done.11.refs_6_
  72.5 10.0 %shard_map.93 = (f32[512,512]{1,0:T(8,128)S(1)}, f32[512,512]{1,0:T(8,128)S(1)}) custom-call(s32[4]{0:T(128)S(1)} %pad_add_fusion.place_ref, bf16[1024,2048]{1,0:T(8,128)(2,1)S(1)} %shard_map.92.x_hbm, f32[8,512]{1,0:T(8,128)S(1)} %bitcast.44, f32[8,512]{1,0:T(8,128)S(1)} %collective-permute-done.3.far_mix_ref, ...), custom_call_target="tpu_custom_call" | custom-call | flops 5368709120 | bytes 9437184 | tf_op jit(solution)/shard_map/pallas_call | solution.py:172
  82.5 0.1 collective-permute-start.13
  82.6 2.6 %collective-permute-done.13 = f32[512,512]{1,0:T(8,128)S(1)} collective-permute-done((f32[512,512]{1,0:T(8,128)S(1)}, f32[512,512]{1,0:T(8,128)S(1)}, u32[]{:S(2)}, u32[]{:S(2)}) %collective-permute-start.13) | collective-permute-done | bytes 1048608 | tf_op jit(solution)/shard_map/ppermute | solution.py:49
  85.3 0.3 add_convert_fusion.refs_0_
  85.5 2.6 %collective-permute-start.14 = (bf16[512,512]{1,0:T(8,128)(2,1)S(1)}, bf16[512,512]{1,0:T(8,128)(2,1)S(1)}, u32[]{:S(2)}, u32[]{:S(2)}) collective-permute-start(bf16[512,512]{1,0:T(8,128)(2,1)S(1)} %add_convert_fusion.refs_0_), channel_id=1, source_target_pairs={{0,1},{1,0},{2,3},{3,2},{4,5},{5,4},{6,7},{7,6},{8,9},{9,8},{10,11... | collective-permute-start | bytes 1572872 | tf_op jit(solution)/shard_map/ppermute | solution.py:432
  88.1 1.3 collective-permute-start.16
  89.4 3.3 %collective-permute-start.15 = (bf16[512,512]{1,0:T(8,128)(2,1)S(1)}, bf16[512,512]{1,0:T(8,128)(2,1)S(1)}, u32[]{:S(2)}, u32[]{:S(2)}) collective-permute-start(bf16[512,512]{1,0:T(8,128)(2,1)S(1)} %add_convert_fusion.refs_0_), channel_id=1, source_target_pairs={{0,2},{2,4},{4,6},{1,3},{3,5},{5,7},{8,10},{10,12},{12,14},{9,11},... | collective-permute-start | bytes 1572872 | tf_op jit(solution)/shard_map/ppermute | solution.py:433
  92.7 1.5 %collective-permute-start.17 = (bf16[512,512]{1,0:T(8,128)(2,1)S(1)}, bf16[512,512]{1,0:T(8,128)(2,1)}, u32[]{:S(2)}, u32[]{:S(2)}) collective-permute-start(bf16[512,512]{1,0:T(8,128)(2,1)S(1)} %add_convert_fusion.refs_0_), channel_id=1, source_target_pairs={{0,6},{1,7},{8,14},{9,15},{16,22},{17,23},{24,30},{25,31},{32,38},... | collective-permute-start | bytes 1572872 | tf_op jit(solution)/shard_map/ppermute | solution.py:434
  94.2 7.0 %collective-permute-done.14.refs_1_ = bf16[512,512]{1,0:T(8,128)(2,1)S(1)} collective-permute-done((bf16[512,512]{1,0:T(8,128)(2,1)S(1)}, bf16[512,512]{1,0:T(8,128)(2,1)S(1)}, u32[]{:S(2)}, u32[]{:S(2)}) %collective-permute-start.14) | collective-permute-done | bytes 524320 | tf_op jit(solution)/shard_map/ppermute | solution.py:432
  101.2 3.8 %collective-permute-start.18 = (bf16[512,512]{1,0:T(8,128)(2,1)S(1)}, bf16[512,512]{1,0:T(8,128)(2,1)S(1)}, u32[]{:S(2)}, u32[]{:S(2)}) collective-permute-start(bf16[512,512]{1,0:T(8,128)(2,1)S(1)} %collective-permute-done.14.refs_1_), channel_id=1, source_target_pairs={{0,2},{2,4},{4,6},{1,3},{3,5},{5,7},{8,10},{10,12},{12,14},{9,11},... | collective-permute-start | bytes 1572872 | tf_op jit(solution)/shard_map/ppermute | solution.py:436
  105.0 0.7 collective-permute-start.20
  105.7 0.7 collective-permute-done.16.refs_3_
  106.4 1.3 collective-permute-start.19
  107.8 0.0 all-gather.3.cloned.1.call-done
  107.8 0.0 copy-start.1
  107.8 2.2 %copy-done.1 = bf16[1,512,4096]{2,1,0:T(8,128)(2,1)S(1)} copy-done((bf16[1,512,4096]{2,1,0:T(8,128)(2,1)S(1)}, bf16[1,512,4096]{2,1,0:T(8,128)(2,1)}, u32[]{:S(2)}) %copy-start.1) | copy-done | bytes 4194328
  110.0 4.0 %copy-done.2 = bf16[32,1280,128]{2,1,0:T(8,128)(2,1)S(1)} copy-done((bf16[32,1280,128]{2,1,0:T(8,128)(2,1)S(1)}, bf16[32,1280,128]{2,1,0:T(8,128)(2,1)}, u32[]{:S(2)}) %copy-start.2) | copy-done | bytes 10485784
  114.0 2.5 %shard_map.91.q_ref = bf16[512,256]{1,0:T(8,128)(2,1)S(1)} custom-call(bf16[512,4096]{1,0:T(8,128)(2,1)S(1)} %bitcast.39, bf16[16,2,1280,128]{3,2,1,0:T(8,128)(2,1)S(1)} %bitcast.40), custom_call_target="tpu_custom_call" | custom-call | flops 1073741824 | bytes 6291456 | tf_op jit(solution)/shard_map/pallas_call | solution.py:222
  116.5 0.0 collective-permute-done.15.refs_2_
  116.5 0.0 collective-permute-done.17.refs_4_
  116.5 6.3 %shard_map.94 = (f32[2,512]{1,0:T(2,128)S(1)}, f32[2,512]{1,0:T(2,128)S(1)}, f32[256,512]{1,0:T(8,128)S(1)}) custom-call(s32[4]{0:T(128)S(1)} %pad_add_fusion.place_ref, bf16[512,256]{1,0:T(8,128)(2,1)S(1)} %shard_map.91.q_ref, bf16[512,512]{1,0:T(8,128)(2,1)S(1)} %add_convert_fusion.refs_0_, bf16[512,512]{1,0:T(8,128)(2,1)S(1)} %collective-permute-done.14.refs_1_, ...), custom_call_target="tpu_custom_call" | custom-call | flops 1342177280 | bytes 2621440 | tf_op jit(solution)/shard_map/pallas_call | solution.py:362
  122.8 4.8 %collective-permute-done.18.refs_0_ = bf16[512,512]{1,0:T(8,128)(2,1)S(1)} collective-permute-done((bf16[512,512]{1,0:T(8,128)(2,1)S(1)}, bf16[512,512]{1,0:T(8,128)(2,1)S(1)}, u32[]{:S(2)}, u32[]{:S(2)}) %collective-permute-start.18) | collective-permute-done | bytes 524320 | tf_op jit(solution)/shard_map/ppermute | solution.py:436
  127.7 0.0 collective-permute-done.19.refs_1_
  127.7 0.0 collective-permute-done.20.refs_2_
  127.7 10.2 %shard_map.95 = bf16[512,4096]{1,0:T(8,128)(2,1)} custom-call(s32[4]{0:T(128)S(1)} %pad_add_fusion.place_ref, bf16[512,256]{1,0:T(8,128)(2,1)S(1)} %shard_map.91.q_ref, f32[2,512]{1,0:T(2,128)S(1)} %get-tuple-element.16.m_in, f32[2,512]{1,0:T(2,128)S(1)} %get-tuple-element.17.l_in, f32[256,512]{1,0:T(8,128)S(1)} %get-tuple-element.18.acc_in, ...), custom_call_target="tpu_custom_call" | custom-call | flops 5100273664 | bytes 1572864 | tf_op jit(solution)/shard_map/pallas_call | solution.py:379
  (19 shorter events, 0.1 us)
Async XLA Ops:
  6.5 53.9 %copy-start.6 = (bf16[1,512,2,2]{1,3,2,0:T(2,128)(2,1)S(1)}, bf16[1,512,2,2]{1,3,2,0:T(2,128)(2,1)}, u32[]{:S(2)}) copy-start(bf16[1,512,2,2]{1,3,2,0:T(2,128)(2,1)} %param.15) | copy-start | bytes 12292
  6.5 53.9 %copy-start.5 = (s32[1,512,2,2]{1,3,2,0:T(2,128)S(1)}, s32[1,512,2,2]{1,3,2,0:T(2,128)}, u32[]{:S(2)}) copy-start(s32[1,512,2,2]{1,3,2,0:T(2,128)} %param.14) | copy-start | bytes 24580
  6.5 101.2 %all-gather.3.cloned.1.call-start = ((), (), s32[]{:S(2)}) async-start(), calls=%async_computation | async-start | bytes 11141120 | tf_op jit(solution)/shard_map/all_gather | solution.py:427
  8.4 10.7 %collective-permute-start.1 = (bf16[1280,128]{1,0:T(8,128)(2,1)S(1)}, bf16[1280,128]{1,0:T(8,128)(2,1)S(1)}, u32[]{:S(2)}, u32[]{:S(2)}) collective-permute-start(bf16[1280,128]{1,0:T(8,128)(2,1)S(1)} %pad_maximum_fusion.3), channel_id=1, source_target_pairs={{0,128},{128,0},{1,129},{129,1},{2,130},{130,2},{3,131},{131,3},{4... | collective-permute-start | bytes 983048 | tf_op jit(solution)/shard_map/ppermute | solution.py:421
  11.3 16.9 %collective-permute-start = (bf16[128,1280]{1,0:T(8,128)(2,1)S(1)}, bf16[128,1280]{1,0:T(8,128)(2,1)S(1)}, u32[]{:S(2)}, u32[]{:S(2)}) collective-permute-start(bf16[128,1280]{1,0:T(8,128)(2,1)S(1)} %pad_maximum_fusion.4), channel_id=1, source_target_pairs={{0,0},{1,17},{2,34},{3,51},{4,68},{5,85},{6,102},{7,119},{8,8},{9,... | collective-permute-start | bytes 983048 | tf_op jit(solution)/shard_map/ppermute | solution.py:63
  30.2 30.2 %collective-permute-start.2 = (bf16[512,4096]{1,0:T(8,128)(2,1)}, bf16[512,4096]{1,0:T(8,128)(2,1)}, u32[]{:S(2)}, u32[]{:S(2)}) collective-permute-start(bf16[512,4096]{1,0:T(8,128)(2,1)} %bitcast.37), channel_id=1, source_target_pairs={{0,8},{8,0},{1,9},{9,1},{2,10},{10,2},{3,11},{11,3},{4,12},{12,4},... | collective-permute-start | bytes 12582920 | tf_op jit(solution)/shard_map/ppermute | solution.py:49
  30.9 11.6 %collective-permute-start.5 = (bf16[128,1280]{1,0:T(8,128)(2,1)S(1)}, bf16[128,1280]{1,0:T(8,128)(2,1)S(1)}, u32[]{:S(2)}, u32[]{:S(2)}) collective-permute-start(bf16[128,1280]{1,0:T(8,128)(2,1)S(1)} %collective-permute-done), channel_id=1, source_target_pairs={{0,129},{1,128},{2,131},{3,130},{4,133},{5,132},{6,135},{7,134},{8... | collective-permute-start | bytes 983048 | tf_op jit(solution)/shard_map/ppermute | solution.py:39
  32.1 15.4 %collective-permute-start.6 = (bf16[128,1280]{1,0:T(8,128)(2,1)S(1)}, bf16[128,1280]{1,0:T(8,128)(2,1)S(1)}, u32[]{:S(2)}, u32[]{:S(2)}) collective-permute-start(bf16[128,1280]{1,0:T(8,128)(2,1)S(1)} %collective-permute-done), channel_id=1, source_target_pairs={{0,1},{1,0},{2,3},{3,2},{4,5},{5,4},{6,7},{7,6},{8,12},{9,13},{10,... | collective-permute-start | bytes 983048 | tf_op jit(solution)/shard_map/ppermute | solution.py:39
  38.8 8.8 %collective-permute-start.4 = (bf16[128,1280]{1,0:T(8,128)(2,1)S(1)}, bf16[128,1280]{1,0:T(8,128)(2,1)S(1)}, u32[]{:S(2)}, u32[]{:S(2)}) collective-permute-start(bf16[128,1280]{1,0:T(8,128)(2,1)S(1)} %collective-permute-done), channel_id=1, source_target_pairs={{0,128},{1,129},{2,130},{3,131},{4,132},{5,133},{6,134},{7,135},{8... | collective-permute-start | bytes 983048 | tf_op jit(solution)/shard_map/ppermute | solution.py:39
  47.5 10.7 %collective-permute-start.8 = (bf16[2,128,1280]{2,1,0:T(8,128)(2,1)S(1)}, bf16[2,128,1280]{2,1,0:T(8,128)(2,1)S(1)}, u32[]{:S(2)}, u32[]{:S(2)}) collective-permute-start(bf16[2,128,1280]{2,1,0:T(8,128)(2,1)S(1)} %pad_maximum_fusion.2.refs_1_), channel_id=1, source_target_pairs={{0,6},{1,7},{2,0},{3,1},{4,2},{5,3},{6,4},{7,5},{8,137},{9,136},{1... | collective-permute-start | bytes 1966088 | tf_op jit(solution)/shard_map/ppermute | solution.py:39
  47.7 10.7 %collective-permute-start.7 = (bf16[2,128,1280]{2,1,0:T(8,128)(2,1)S(1)}, bf16[2,128,1280]{2,1,0:T(8,128)(2,1)S(1)}, u32[]{:S(2)}, u32[]{:S(2)}) collective-permute-start(bf16[2,128,1280]{2,1,0:T(8,128)(2,1)S(1)} %pad_maximum_fusion.1.refs_0_), channel_id=1, source_target_pairs={{0,2},{1,3},{2,4},{3,5},{4,6},{5,7},{6,0},{7,1},{8,136},{9,137},{1... | collective-permute-start | bytes 1966088 | tf_op jit(solution)/shard_map/ppermute | solution.py:39
  49.8 16.7 %collective-permute-start.10 = (bf16[2,128,1280]{2,1,0:T(8,128)(2,1)S(1)}, bf16[2,128,1280]{2,1,0:T(8,128)(2,1)S(1)}, u32[]{:S(2)}, u32[]{:S(2)}) collective-permute-start(bf16[2,128,1280]{2,1,0:T(8,128)(2,1)S(1)} %pad_maximum_fusion.2.refs_1_), channel_id=1, source_target_pairs={{0,2},{1,3},{2,4},{3,5},{4,6},{5,7},{6,0},{7,1},{8,136},{9,137},{1... | collective-permute-start | bytes 1966088 | tf_op jit(solution)/shard_map/ppermute | solution.py:39
  49.9 16.7 %collective-permute-start.9 = (bf16[2,128,1280]{2,1,0:T(8,128)(2,1)S(1)}, bf16[2,128,1280]{2,1,0:T(8,128)(2,1)}, u32[]{:S(2)}, u32[]{:S(2)}) collective-permute-start(bf16[2,128,1280]{2,1,0:T(8,128)(2,1)S(1)} %pad_maximum_fusion.1.refs_0_), channel_id=1, source_target_pairs={{0,6},{1,7},{2,0},{3,1},{4,2},{5,3},{6,4},{7,5},{8,137},{9,136},{1... | collective-permute-start | bytes 1966088 | tf_op jit(solution)/shard_map/ppermute | solution.py:39
  58.2 14.1 %collective-permute-start.12 = (bf16[2,128,1280]{2,1,0:T(8,128)(2,1)S(1)}, bf16[2,128,1280]{2,1,0:T(8,128)(2,1)}, u32[]{:S(2)}, u32[]{:S(2)}) collective-permute-start(bf16[2,128,1280]{2,1,0:T(8,128)(2,1)S(1)} %collective-permute-done.8.refs_3_), channel_id=1, source_target_pairs={{0,6},{1,7},{2,0},{3,1},{4,2},{5,3},{6,4},{7,5},{8,137},{9,136},{1... | collective-permute-start | bytes 1966088 | tf_op jit(solution)/shard_map/ppermute | solution.py:39
  58.4 14.1 %collective-permute-start.11 = (bf16[2,128,1280]{2,1,0:T(8,128)(2,1)S(1)}, bf16[2,128,1280]{2,1,0:T(8,128)(2,1)}, u32[]{:S(2)}, u32[]{:S(2)}) collective-permute-start(bf16[2,128,1280]{2,1,0:T(8,128)(2,1)S(1)} %collective-permute-done.7.refs_2_), channel_id=1, source_target_pairs={{0,2},{1,3},{2,4},{3,5},{4,6},{5,7},{6,0},{7,1},{8,136},{9,137},{1... | collective-permute-start | bytes 1966088 | tf_op jit(solution)/shard_map/ppermute | solution.py:39
  60.5 6.1 %collective-permute-start.3 = (f32[8,512]{1,0:T(8,128)S(1)}, f32[8,512]{1,0:T(8,128)S(1)}, u32[]{:S(2)}, u32[]{:S(2)}) collective-permute-start(f32[8,512]{1,0:T(8,128)S(1)} %bitcast.43), channel_id=1, source_target_pairs={{0,8},{8,0},{1,9},{9,1},{2,10},{10,2},{3,11},{11,3},{4,12},{12,4},... | collective-permute-start | bytes 49160 | tf_op jit(solution)/shard_map/ppermute | solution.py:49
  60.8 2.3 %copy-start = (bf16[1,512,4096]{2,1,0:T(8,128)(2,1)S(1)}, bf16[1,512,4096]{2,1,0:T(8,128)(2,1)}, u32[]{:S(2)}) copy-start(bf16[1,512,4096]{2,1,0:T(8,128)(2,1)} %param.9) | copy-start | bytes 12582916
  66.5 41.2 %copy-start.7 = (bf16[1,512,2,2]{1,3,2,0:T(2,128)(2,1)S(1)}, bf16[1,512,2,2]{1,3,2,0:T(2,128)(2,1)}, u32[]{:S(2)}) copy-start(bf16[1,512,2,2]{1,3,2,0:T(2,128)(2,1)} %param.17) | copy-start | bytes 12292
  66.5 41.2 %copy-start.4 = (s32[1,512,2,2]{1,3,2,0:T(2,128)S(1)}, s32[1,512,2,2]{1,3,2,0:T(2,128)}, u32[]{:S(2)}) copy-start(s32[1,512,2,2]{1,3,2,0:T(2,128)} %param.16) | copy-start | bytes 24580
  82.5 2.7 %collective-permute-start.13 = (f32[512,512]{1,0:T(8,128)S(1)}, f32[512,512]{1,0:T(8,128)S(1)}, u32[]{:S(2)}, u32[]{:S(2)}) collective-permute-start(f32[512,512]{1,0:T(8,128)S(1)} %get-tuple-element.15), channel_id=1, source_target_pairs={{0,8},{8,0},{1,9},{9,1},{2,10},{10,2},{3,11},{11,3},{4,12},{12,4},... | collective-permute-start | bytes 3145736 | tf_op jit(solution)/shard_map/ppermute | solution.py:49
  85.5 15.7 %collective-permute-start.14 = (bf16[512,512]{1,0:T(8,128)(2,1)S(1)}, bf16[512,512]{1,0:T(8,128)(2,1)S(1)}, u32[]{:S(2)}, u32[]{:S(2)}) collective-permute-start(bf16[512,512]{1,0:T(8,128)(2,1)S(1)} %add_convert_fusion.refs_0_), channel_id=1, source_target_pairs={{0,1},{1,0},{2,3},{3,2},{4,5},{5,4},{6,7},{7,6},{8,9},{9,8},{10,11... | collective-permute-start | bytes 1572872 | tf_op jit(solution)/shard_map/ppermute | solution.py:432
  88.1 18.2 %collective-permute-start.16 = (bf16[512,512]{1,0:T(8,128)(2,1)S(1)}, bf16[512,512]{1,0:T(8,128)(2,1)S(1)}, u32[]{:S(2)}, u32[]{:S(2)}) collective-permute-start(bf16[512,512]{1,0:T(8,128)(2,1)S(1)} %add_convert_fusion.refs_0_), channel_id=1, source_target_pairs={{0,4},{2,6},{1,5},{3,7},{8,12},{10,14},{9,13},{11,15},{16,20},{18,... | collective-permute-start | bytes 1572872 | tf_op jit(solution)/shard_map/ppermute | solution.py:435
  89.4 27.1 %collective-permute-start.15 = (bf16[512,512]{1,0:T(8,128)(2,1)S(1)}, bf16[512,512]{1,0:T(8,128)(2,1)S(1)}, u32[]{:S(2)}, u32[]{:S(2)}) collective-permute-start(bf16[512,512]{1,0:T(8,128)(2,1)S(1)} %add_convert_fusion.refs_0_), channel_id=1, source_target_pairs={{0,2},{2,4},{4,6},{1,3},{3,5},{5,7},{8,10},{10,12},{12,14},{9,11},... | collective-permute-start | bytes 1572872 | tf_op jit(solution)/shard_map/ppermute | solution.py:433
  92.7 23.8 %collective-permute-start.17 = (bf16[512,512]{1,0:T(8,128)(2,1)S(1)}, bf16[512,512]{1,0:T(8,128)(2,1)}, u32[]{:S(2)}, u32[]{:S(2)}) collective-permute-start(bf16[512,512]{1,0:T(8,128)(2,1)S(1)} %add_convert_fusion.refs_0_), channel_id=1, source_target_pairs={{0,6},{1,7},{8,14},{9,15},{16,22},{17,23},{24,30},{25,31},{32,38},... | collective-permute-start | bytes 1572872 | tf_op jit(solution)/shard_map/ppermute | solution.py:434
  101.2 26.5 %collective-permute-start.18 = (bf16[512,512]{1,0:T(8,128)(2,1)S(1)}, bf16[512,512]{1,0:T(8,128)(2,1)S(1)}, u32[]{:S(2)}, u32[]{:S(2)}) collective-permute-start(bf16[512,512]{1,0:T(8,128)(2,1)S(1)} %collective-permute-done.14.refs_1_), channel_id=1, source_target_pairs={{0,2},{2,4},{4,6},{1,3},{3,5},{5,7},{8,10},{10,12},{12,14},{9,11},... | collective-permute-start | bytes 1572872 | tf_op jit(solution)/shard_map/ppermute | solution.py:436
  105.0 22.7 %collective-permute-start.20 = (bf16[512,512]{1,0:T(8,128)(2,1)S(1)}, bf16[512,512]{1,0:T(8,128)(2,1)S(1)}, u32[]{:S(2)}, u32[]{:S(2)}) collective-permute-start(bf16[512,512]{1,0:T(8,128)(2,1)S(1)} %collective-permute-done.14.refs_1_), channel_id=1, source_target_pairs={{0,6},{1,7},{8,14},{9,15},{16,22},{17,23},{24,30},{25,31},{32,38},... | collective-permute-start | bytes 1572872 | tf_op jit(solution)/shard_map/ppermute | solution.py:437
  106.4 21.3 %collective-permute-start.19 = (bf16[512,512]{1,0:T(8,128)(2,1)S(1)}, bf16[512,512]{1,0:T(8,128)(2,1)}, u32[]{:S(2)}, u32[]{:S(2)}) collective-permute-start(bf16[512,512]{1,0:T(8,128)(2,1)S(1)} %collective-permute-done.16.refs_3_), channel_id=1, source_target_pairs={{0,1},{1,0},{2,3},{3,2},{4,5},{5,4},{6,7},{7,6},{8,9},{9,8},{10,11... | collective-permute-start | bytes 1572872 | tf_op jit(solution)/shard_map/ppermute | solution.py:438
  107.8 2.2 %copy-start.1 = (bf16[1,512,4096]{2,1,0:T(8,128)(2,1)S(1)}, bf16[1,512,4096]{2,1,0:T(8,128)(2,1)}, u32[]{:S(2)}) copy-start(bf16[1,512,4096]{2,1,0:T(8,128)(2,1)} %param.9) | copy-start | bytes 12582916
  110.0 4.0 %copy-start.2 = (bf16[32,1280,128]{2,1,0:T(8,128)(2,1)S(1)}, bf16[32,1280,128]{2,1,0:T(8,128)(2,1)}, u32[]{:S(2)}) copy-start(bf16[32,1280,128]{2,1,0:T(8,128)(2,1)} %all-gather.3.cloned.1.call-done) | copy-start | bytes 31457284
  114.0 13.7 %copy-start.3 = (bf16[32,1280,128]{2,1,0:T(8,128)(2,1)S(1)}, bf16[32,1280,128]{2,1,0:T(8,128)(2,1)}, u32[]{:S(2)}) copy-start(bf16[32,1280,128]{2,1,0:T(8,128)(2,1)} %all-gather.3.cloned.1.call-done) | copy-start | bytes 31457284
Sparse Core Ops, SparseCore 0:
  30.3 69.1 all-gather.2

commit v2 on v1

--- a/solution.py
+++ b/solution.py
@@ -80,11 +80,20 @@
 
 def pack_kernel(place_ref, own_ref, other_ref, out_ref):
     rows = own_ref.shape[0]
-    core = place_ref[3]
-    for i in range(SIZES[0] * SIZES[1]):
-        lanes = pl.ds(pl.multiple_of((SIZES[2] * i + core) * DH, DH), DH)
-        out_ref[:rows, i * DH : (i + 1) * DH] = own_ref[:, lanes]
-        out_ref[rows:, i * DH : (i + 1) * DH] = other_ref[:, lanes]
+    chip_x, chip_y, level, core = (place_ref[i] for i in range(4))
+    for i, (second, pair) in enumerate(GROUPS):
+        for j, first in enumerate(FIRST[pair]):
+            by_x = jnp.where(core == 0, first, second)
+            by_y = jnp.where(core == 0, second, first)
+            from_x = lax.rem(chip_x + by_x + RING, RING)
+            from_y = lax.rem(chip_y + by_y + RING, RING)
+            by = from_y * SIZES[4] + lax.div(from_x, 2)
+            from_z = lax.rem(level + jnp.where(core == 0, SIZES[1] - by, by), SIZES[1])
+            shard = (lax.rem(from_x, 2) * SIZES[1] + from_z) * SIZES[2] + core
+            lanes = pl.ds(pl.multiple_of(shard * DH, DH), DH)
+            to = slice((2 * i + j) * DH, (2 * i + j + 1) * DH)
+            out_ref[:rows, to] = own_ref[:, lanes]
+            out_ref[rows:, to] = other_ref[:, lanes]
 
 
 def packed(place, own, other):
@@ -102,56 +111,23 @@
     )(place, own, other)
 
 
-HALVES = ((0, 512), (512, 768))
-
-
-def project_kernel(count, place_ref, x_hbm, mix_ref, far_mix_ref, *refs):
+def project_kernel(count, place_ref, x_ref, mix_ref, far_mix_ref, *refs):
     pieces = refs[:count]
-    own_ref, other_ref, x_ref, w_ref, x_sem, w_sem = refs[count:]
-    chip_x, chip_y, level, core = (place_ref[i] for i in range(4))
-    rows = own_ref.shape[0]
-    x_copy = pltpu.make_async_copy(x_hbm, x_ref, x_sem)
-    w_copies = [[] for _ in HALVES]
-    for i, piece in enumerate(pieces):
-        second, pair = GROUPS[i]
-        for j, first in enumerate(FIRST[pair]):
-            by_x = jnp.where(core == 0, first, second)
-            by_y = jnp.where(core == 0, second, first)
-            from_x = lax.rem(chip_x + by_x + RING, RING)
-            from_y = lax.rem(chip_y + by_y + RING, RING)
-            by = from_y * SIZES[4] + lax.div(from_x, 2)
-            from_z = lax.rem(level + jnp.where(core == 0, SIZES[1] - by, by), SIZES[1])
-            shard = lax.rem(from_x, 2) * SIZES[1] + from_z
-            for h, (start, size) in enumerate(HALVES):
-                columns = pl.ds(start, size)
-                w_copies[h].append(
-                    pltpu.make_async_copy(
-                        piece.at[j, :, columns], w_ref.at[shard, :, columns], w_sem.at[h]
-                    )
-                )
-    for copy in w_copies[0]:
-        copy.start()
-    x_copy.start()
-    for copy in w_copies[1]:
-        copy.start()
+    outs = refs[count:]
+    rows = outs[0].shape[0]
     mixes = (jnp.transpose(mix_ref[...]), jnp.transpose(far_mix_ref[...]))
-    x_copy.wait()
-    for copy in w_copies[0]:
-        copy.wait()
 
     def product(column):
-        w = w_ref[:, :, column : column + WIDTH].reshape(x_ref.shape[1], WIDTH)
+        w = jnp.concatenate(
+            [piece[j, :, column : column + WIDTH] for piece in pieces for j in range(2)], axis=0
+        )
         block = jnp.dot(x_ref[...], w, preferred_element_type=jnp.float32)
         return block[:rows], block[rows:]
 
-    outs = (own_ref, other_ref)
     for out, block in zip(outs, product(0)):
         out[:, :WIDTH] = block
     for head in range(HEADS):
         for half in range(EXPERTS // 2):
-            if head == 0 and half == 1:
-                for copy in w_copies[1]:
-                    copy.wait()
             expert = head * EXPERTS + 2 * half
             lanes = slice(WIDTH + head * DH, WIDTH + (head + 1) * DH)
             for out, mix, block in zip(outs, mixes, product(WIDTH + expert * DH)):
@@ -166,21 +142,13 @@
     rows = x.shape[0] // 2
     depth = x.shape[1]
     _, shard, columns = pieces[0].shape
-    any_space = pl.BlockSpec(memory_space=pl.ANY)
     vmem = pl.BlockSpec(memory_space=pltpu.VMEM)
     count = len(pieces)
     return pl.pallas_call(
         functools.partial(project_kernel, count),
-        in_specs=[pl.BlockSpec(memory_space=pltpu.SMEM), any_space, vmem, vmem]
-        + [any_space] * count,
+        in_specs=[pl.BlockSpec(memory_space=pltpu.SMEM)] + [vmem] * (3 + count),
         out_specs=[vmem, vmem],
         out_shape=[jax.ShapeDtypeStruct((rows, 2 * WIDTH), jnp.float32)] * 2,
-        scratch_shapes=[
-            pltpu.VMEM(x.shape, x.dtype),
-            pltpu.VMEM((2 * count, shard, columns), jnp.bfloat16),
-            pltpu.SemaphoreType.DMA,
-            pltpu.SemaphoreType.DMA((len(HALVES),)),
-        ],
         compiler_params=VM,
         cost_estimate=pl.CostEstimate(
             flops=4 * rows * depth * columns,

time: 147 us -> 145 us (0.986)
  Pallas kernels: 32.4 us -> 29.7 us
    pallas_call x1, Pallas kernels: 9.98 us -> 7.22 us  [project(): pl.pallas_call(functools.partial(project_kernel, count), in_specs=[pl.Blo...]
  transfers between devices with their start and end apart: 22 -> 22, of which waited for: 11 -> 11; matrix products, arithmetic and copies ran while one was open for 2% -> 2% of each run, Pallas kernels for 15% -> 14%
where the time goes in v2:
time: 145 us; the launch traced here: 142 us
  waiting for transfers between devices  43.9 us (30%)
  starting transfers between devices  39.8 us (27%)
  Pallas kernels  29.7 us (20%)
  between operations  13.7 us (9%)
  local copies, waits for them, and re-layouts  11.3 us (8%)
  other arithmetic  3.49 us (2%)
    ppermute x9, waiting for transfers between devices, moved(): return lax.ppermute(x, AXES, pairs)  20 us
    ppermute x9, starting transfers between devices, moved(): return lax.ppermute(x, AXES, pairs)  15.3 us
    pallas_call x1, Pallas kernels, attend_late(): pl.pallas_call(functools.partial(attend_late_kernel, needs), in_specs=[pl...  10.2 us
    unnamed x18, local copies, waits for them, and re-layouts  10.2 us
    ppermute x1, waiting for transfers between devices, lifted(): return lax.ppermute(x, AXES, pairs)  9.13 us
    ppermute x1, starting transfers between devices, lifted(): return lax.ppermute(x, AXES, pairs)  7.75 us
    pallas_call x1, Pallas kernels, project(): pl.pallas_call(functools.partial(project_kernel, count), in_specs=[pl.Blo...  7.22 us
    ppermute x1, waiting for transfers between devices, on_device(): other = lax.ppermute(own, 'x_hi', [(0, 1), (1, 0)])  6.92 us
  transfers between devices with their start and end apart: 22, of which 11 were waited for; matrix products, arithmetic and copies ran while one was open for 2% of the time, Pallas kernels for 14%

profile of v2, /device:TPU:54, one launch (start us, length us, event | category | flops | bytes accessed | tf_op | source)
XLA Modules:
  0.0 141.9 jit_solution(16090575614722475201)
XLA Ops:
  6.5 0.9 copy.24
  7.4 1.0 pad_maximum_fusion.3
  8.4 0.9 collective-permute-start.1
  9.3 1.1 reshape.38
  10.4 0.9 copy.27
  11.3 7.8 %collective-permute-start = (bf16[128,1280]{1,0:T(8,128)(2,1)S(1)}, bf16[128,1280]{1,0:T(8,128)(2,1)S(1)}, u32[]{:S(2)}, u32[]{:S(2)}) collective-permute-start(bf16[128,1280]{1,0:T(8,128)(2,1)S(1)} %pad_maximum_fusion.4), channel_id=1, source_target_pairs={{0,0},{1,17},{2,34},{3,51},{4,68},{5,85},{6,102},{7,119},{8,8},{9,... | collective-permute-start | bytes 983048 | tf_op jit(solution)/shard_map/ppermute | solution.py:63
  19.1 0.0 collective-permute-done.1
  19.1 9.1 %collective-permute-done = bf16[128,1280]{1,0:T(8,128)(2,1)S(1)} collective-permute-done((bf16[128,1280]{1,0:T(8,128)(2,1)S(1)}, bf16[128,1280]{1,0:T(8,128)(2,1)S(1)}, u32[]{:S(2)}, u32[]{:S(2)}) %collective-permute-start) | collective-permute-done | bytes 327712 | tf_op jit(solution)/shard_map/ppermute | solution.py:63
  28.2 1.1 select_bitcast_fusion.1
  29.3 0.9 pad_maximum_fusion
  30.2 0.0 all-gather.3.cloned.1.call-update
  30.2 0.7 collective-permute-start.2
  30.9 1.2 collective-permute-start.5
  32.1 6.8 %collective-permute-start.6 = (bf16[128,1280]{1,0:T(8,128)(2,1)S(1)}, bf16[128,1280]{1,0:T(8,128)(2,1)S(1)}, u32[]{:S(2)}, u32[]{:S(2)}) collective-permute-start(bf16[128,1280]{1,0:T(8,128)(2,1)S(1)} %collective-permute-done), channel_id=1, source_target_pairs={{0,1},{1,0},{2,3},{3,2},{4,5},{5,4},{6,7},{7,6},{8,12},{9,13},{10,... | collective-permute-start | bytes 983048 | tf_op jit(solution)/shard_map/ppermute | solution.py:39
  38.8 1.1 collective-permute-start.4
  40.0 2.5 %collective-permute-done.5 = bf16[128,1280]{1,0:T(8,128)(2,1)S(1)} collective-permute-done((bf16[128,1280]{1,0:T(8,128)(2,1)S(1)}, bf16[128,1280]{1,0:T(8,128)(2,1)S(1)}, u32[]{:S(2)}, u32[]{:S(2)}) %collective-permute-start.5) | collective-permute-done | bytes 327712 | tf_op jit(solution)/shard_map/ppermute | solution.py:39
  42.4 5.1 %collective-permute-done.6 = bf16[128,1280]{1,0:T(8,128)(2,1)S(1)} collective-permute-done((bf16[128,1280]{1,0:T(8,128)(2,1)S(1)}, bf16[128,1280]{1,0:T(8,128)(2,1)S(1)}, u32[]{:S(2)}, u32[]{:S(2)}) %collective-permute-start.6) | collective-permute-done | bytes 327712 | tf_op jit(solution)/shard_map/ppermute | solution.py:39
  47.5 0.1 pad_maximum_fusion.2.refs_1_
  47.5 0.1 collective-permute-start.8
  47.6 0.0 collective-permute-done.4
  47.7 0.1 pad_maximum_fusion.1.refs_0_
  47.7 2.1 %collective-permute-start.7 = (bf16[2,128,1280]{2,1,0:T(8,128)(2,1)S(1)}, bf16[2,128,1280]{2,1,0:T(8,128)(2,1)S(1)}, u32[]{:S(2)}, u32[]{:S(2)}) collective-permute-start(bf16[2,128,1280]{2,1,0:T(8,128)(2,1)S(1)} %pad_maximum_fusion.1.refs_0_), channel_id=1, source_target_pairs={{0,2},{1,3},{2,4},{3,5},{4,6},{5,7},{6,0},{7,1},{8,136},{9,137},{1... | collective-permute-start | bytes 1966088 | tf_op jit(solution)/shard_map/ppermute | solution.py:39
  49.8 0.1 collective-permute-start.10
  49.9 1.9 %collective-permute-start.9 = (bf16[2,128,1280]{2,1,0:T(8,128)(2,1)S(1)}, bf16[2,128,1280]{2,1,0:T(8,128)(2,1)}, u32[]{:S(2)}, u32[]{:S(2)}) collective-permute-start(bf16[2,128,1280]{2,1,0:T(8,128)(2,1)S(1)} %pad_maximum_fusion.1.refs_0_), channel_id=1, source_target_pairs={{0,6},{1,7},{2,0},{3,1},{4,2},{5,3},{6,4},{7,5},{8,137},{9,136},{1... | collective-permute-start | bytes 1966088 | tf_op jit(solution)/shard_map/ppermute | solution.py:39
  51.8 6.4 %collective-permute-done.8.refs_3_ = bf16[2,128,1280]{2,1,0:T(8,128)(2,1)S(1)} collective-permute-done((bf16[2,128,1280]{2,1,0:T(8,128)(2,1)S(1)}, bf16[2,128,1280]{2,1,0:T(8,128)(2,1)S(1)}, u32[]{:S(2)}, u32[]{:S(2)}) %collective-permute-start.8) | collective-permute-done | bytes 655392 | tf_op jit(solution)/shard_map/ppermute | solution.py:39
  58.2 0.0 collective-permute-start.12
  58.2 0.2 collective-permute-done.7.refs_2_
  58.4 2.0 %collective-permute-start.11 = (bf16[2,128,1280]{2,1,0:T(8,128)(2,1)S(1)}, bf16[2,128,1280]{2,1,0:T(8,128)(2,1)}, u32[]{:S(2)}, u32[]{:S(2)}) collective-permute-start(bf16[2,128,1280]{2,1,0:T(8,128)(2,1)S(1)} %collective-permute-done.7.refs_2_), channel_id=1, source_target_pairs={{0,2},{1,3},{2,4},{3,5},{4,6},{5,7},{6,0},{7,1},{8,136},{9,137},{1... | collective-permute-start | bytes 1966088 | tf_op jit(solution)/shard_map/ppermute | solution.py:39
  60.4 0.0 collective-permute-done.2.other_ref
  60.5 0.3 collective-permute-start.3
  60.7 0.1 pad_add_fusion.place_ref
  60.8 2.3 %copy-done = bf16[1,512,4096]{2,1,0:T(8,128)(2,1)S(1)} copy-done((bf16[1,512,4096]{2,1,0:T(8,128)(2,1)S(1)}, bf16[1,512,4096]{2,1,0:T(8,128)(2,1)}, u32[]{:S(2)}) %copy-start) | copy-done | bytes 4194328
  63.1 3.5 %shard_map.92.x_ref = bf16[1024,2048]{1,0:T(8,128)(2,1)S(1)} custom-call(s32[4]{0:T(128)S(1)} %pad_add_fusion.place_ref, bf16[512,4096]{1,0:T(8,128)(2,1)S(1)} %bitcast.38, bf16[512,4096]{1,0:T(8,128)(2,1)} %collective-permute-done.2.other_ref), custom_call_target="tpu_custom_call" | custom-call | bytes 12582912 | tf_op jit(solution)/shard_map/pallas_call | solution.py:102
  66.6 0.0 copy-start.7
  66.6 0.0 copy-start.4
  66.6 0.0 collective-permute-done.3.far_mix_ref
  66.6 0.0 collective-permute-done.10.refs_5_
  66.6 5.7 %collective-permute-done.12.refs_7_ = bf16[2,128,1280]{2,1,0:T(8,128)(2,1)} collective-permute-done((bf16[2,128,1280]{2,1,0:T(8,128)(2,1)S(1)}, bf16[2,128,1280]{2,1,0:T(8,128)(2,1)}, u32[]{:S(2)}, u32[]{:S(2)}) %collective-permute-start.12) | collective-permute-done | bytes 655392 | tf_op jit(solution)/shard_map/ppermute | solution.py:39
  72.4 0.2 collective-permute-done.11.refs_6_
  72.5 7.2 %shard_map.93 = (f32[512,512]{1,0:T(8,128)S(1)}, f32[512,512]{1,0:T(8,128)S(1)}) custom-call(s32[4]{0:T(128)S(1)} %pad_add_fusion.place_ref, bf16[1024,2048]{1,0:T(8,128)(2,1)S(1)} %shard_map.92.x_ref, f32[8,512]{1,0:T(8,128)S(1)} %bitcast.44, f32[8,512]{1,0:T(8,128)S(1)} %collective-permute-done.3.far_mix_ref, ...), custom_call_target="tpu_custom_call" | custom-call | flops 5368709120 | bytes 9437184 | tf_op jit(solution)/shard_map/pallas_call | solution.py:147
  79.8 0.1 collective-permute-start.13
  79.9 2.6 %collective-permute-done.13 = f32[512,512]{1,0:T(8,128)S(1)} collective-permute-done((f32[512,512]{1,0:T(8,128)S(1)}, f32[512,512]{1,0:T(8,128)S(1)}, u32[]{:S(2)}, u32[]{:S(2)}) %collective-permute-start.13) | collective-permute-done | bytes 1048608 | tf_op jit(solution)/shard_map/ppermute | solution.py:49
  82.5 0.3 add_convert_fusion.refs_0_
  82.8 2.5 %collective-permute-start.14 = (bf16[512,512]{1,0:T(8,128)(2,1)S(1)}, bf16[512,512]{1,0:T(8,128)(2,1)S(1)}, u32[]{:S(2)}, u32[]{:S(2)}) collective-permute-start(bf16[512,512]{1,0:T(8,128)(2,1)S(1)} %add_convert_fusion.refs_0_), channel_id=1, source_target_pairs={{0,1},{1,0},{2,3},{3,2},{4,5},{5,4},{6,7},{7,6},{8,9},{9,8},{10,11... | collective-permute-start | bytes 1572872 | tf_op jit(solution)/shard_map/ppermute | solution.py:400
  85.3 1.3 collective-permute-start.16
  86.6 3.3 %collective-permute-start.15 = (bf16[512,512]{1,0:T(8,128)(2,1)S(1)}, bf16[512,512]{1,0:T(8,128)(2,1)S(1)}, u32[]{:S(2)}, u32[]{:S(2)}) collective-permute-start(bf16[512,512]{1,0:T(8,128)(2,1)S(1)} %add_convert_fusion.refs_0_), channel_id=1, source_target_pairs={{0,2},{2,4},{4,6},{1,3},{3,5},{5,7},{8,10},{10,12},{12,14},{9,11},... | collective-permute-start | bytes 1572872 | tf_op jit(solution)/shard_map/ppermute | solution.py:401
  89.9 1.5 %collective-permute-start.17 = (bf16[512,512]{1,0:T(8,128)(2,1)S(1)}, bf16[512,512]{1,0:T(8,128)(2,1)}, u32[]{:S(2)}, u32[]{:S(2)}) collective-permute-start(bf16[512,512]{1,0:T(8,128)(2,1)S(1)} %add_convert_fusion.refs_0_), channel_id=1, source_target_pairs={{0,6},{1,7},{8,14},{9,15},{16,22},{17,23},{24,30},{25,31},{32,38},... | collective-permute-start | bytes 1572872 | tf_op jit(solution)/shard_map/ppermute | solution.py:402
  91.4 6.9 %collective-permute-done.14.refs_1_ = bf16[512,512]{1,0:T(8,128)(2,1)S(1)} collective-permute-done((bf16[512,512]{1,0:T(8,128)(2,1)S(1)}, bf16[512,512]{1,0:T(8,128)(2,1)S(1)}, u32[]{:S(2)}, u32[]{:S(2)}) %collective-permute-start.14) | collective-permute-done | bytes 524320 | tf_op jit(solution)/shard_map/ppermute | solution.py:400
  98.3 4.1 %collective-permute-start.18 = (bf16[512,512]{1,0:T(8,128)(2,1)S(1)}, bf16[512,512]{1,0:T(8,128)(2,1)S(1)}, u32[]{:S(2)}, u32[]{:S(2)}) collective-permute-start(bf16[512,512]{1,0:T(8,128)(2,1)S(1)} %collective-permute-done.14.refs_1_), channel_id=1, source_target_pairs={{0,2},{2,4},{4,6},{1,3},{3,5},{5,7},{8,10},{10,12},{12,14},{9,11},... | collective-permute-start | bytes 1572872 | tf_op jit(solution)/shard_map/ppermute | solution.py:404
  102.4 0.7 collective-permute-start.20
  103.1 0.4 collective-permute-done.16.refs_3_
  103.5 1.4 collective-permute-start.19
  105.0 0.0 all-gather.3.cloned.1.call-done
  105.0 0.0 copy-start.1
  105.0 2.2 %copy-done.1 = bf16[1,512,4096]{2,1,0:T(8,128)(2,1)S(1)} copy-done((bf16[1,512,4096]{2,1,0:T(8,128)(2,1)S(1)}, bf16[1,512,4096]{2,1,0:T(8,128)(2,1)}, u32[]{:S(2)}) %copy-start.1) | copy-done | bytes 4194328
  107.2 4.0 %copy-done.2 = bf16[32,1280,128]{2,1,0:T(8,128)(2,1)S(1)} copy-done((bf16[32,1280,128]{2,1,0:T(8,128)(2,1)S(1)}, bf16[32,1280,128]{2,1,0:T(8,128)(2,1)}, u32[]{:S(2)}) %copy-start.2) | copy-done | bytes 10485784
  111.2 2.5 %shard_map.91.q_ref = bf16[512,256]{1,0:T(8,128)(2,1)S(1)} custom-call(bf16[512,4096]{1,0:T(8,128)(2,1)S(1)} %bitcast.39, bf16[16,2,1280,128]{3,2,1,0:T(8,128)(2,1)S(1)} %bitcast.40), custom_call_target="tpu_custom_call" | custom-call | flops 1073741824 | bytes 6291456 | tf_op jit(solution)/shard_map/pallas_call | solution.py:190
  113.7 0.0 collective-permute-done.15.refs_2_
  113.7 0.0 collective-permute-done.17.refs_4_
  113.7 6.3 %shard_map.94 = (f32[2,512]{1,0:T(2,128)S(1)}, f32[2,512]{1,0:T(2,128)S(1)}, f32[256,512]{1,0:T(8,128)S(1)}) custom-call(s32[4]{0:T(128)S(1)} %pad_add_fusion.place_ref, bf16[512,256]{1,0:T(8,128)(2,1)S(1)} %shard_map.91.q_ref, bf16[512,512]{1,0:T(8,128)(2,1)S(1)} %add_convert_fusion.refs_0_, bf16[512,512]{1,0:T(8,128)(2,1)S(1)} %collective-permute-done.14.refs_1_, ...), custom_call_target="tpu_custom_call" | custom-call | flops 1342177280 | bytes 2621440 | tf_op jit(solution)/shard_map/pallas_call | solution.py:330
  120.1 4.8 %collective-permute-done.18.refs_0_ = bf16[512,512]{1,0:T(8,128)(2,1)S(1)} collective-permute-done((bf16[512,512]{1,0:T(8,128)(2,1)S(1)}, bf16[512,512]{1,0:T(8,128)(2,1)S(1)}, u32[]{:S(2)}, u32[]{:S(2)}) %collective-permute-start.18) | collective-permute-done | bytes 524320 | tf_op jit(solution)/shard_map/ppermute | solution.py:404
  124.8 0.0 collective-permute-done.19.refs_1_
  124.9 0.0 collective-permute-done.20.refs_2_
  124.9 10.2 %shard_map.95 = bf16[512,4096]{1,0:T(8,128)(2,1)} custom-call(s32[4]{0:T(128)S(1)} %pad_add_fusion.place_ref, bf16[512,256]{1,0:T(8,128)(2,1)S(1)} %shard_map.91.q_ref, f32[2,512]{1,0:T(2,128)S(1)} %get-tuple-element.16.m_in, f32[2,512]{1,0:T(2,128)S(1)} %get-tuple-element.17.l_in, f32[256,512]{1,0:T(8,128)S(1)} %get-tuple-element.18.acc_in, ...), custom_call_target="tpu_custom_call" | custom-call | flops 5100273664 | bytes 1572864 | tf_op jit(solution)/shard_map/pallas_call | solution.py:347
  (19 shorter events, 0.1 us)
Async XLA Ops:
  6.5 53.9 %copy-start.6 = (bf16[1,512,2,2]{1,3,2,0:T(2,128)(2,1)S(1)}, bf16[1,512,2,2]{1,3,2,0:T(2,128)(2,1)}, u32[]{:S(2)}) copy-start(bf16[1,512,2,2]{1,3,2,0:T(2,128)(2,1)} %param.15) | copy-start | bytes 12292
  6.5 53.9 %copy-start.5 = (s32[1,512,2,2]{1,3,2,0:T(2,128)S(1)}, s32[1,512,2,2]{1,3,2,0:T(2,128)}, u32[]{:S(2)}) copy-start(s32[1,512,2,2]{1,3,2,0:T(2,128)} %param.14) | copy-start | bytes 24580
  6.5 98.5 %all-gather.3.cloned.1.call-start = ((), (), s32[]{:S(2)}) async-start(), calls=%async_computation | async-start | bytes 11141120 | tf_op jit(solution)/shard_map/all_gather | solution.py:395
  8.4 10.7 %collective-permute-start.1 = (bf16[1280,128]{1,0:T(8,128)(2,1)S(1)}, bf16[1280,128]{1,0:T(8,128)(2,1)S(1)}, u32[]{:S(2)}, u32[]{:S(2)}) collective-permute-start(bf16[1280,128]{1,0:T(8,128)(2,1)S(1)} %pad_maximum_fusion.3), channel_id=1, source_target_pairs={{0,128},{128,0},{1,129},{129,1},{2,130},{130,2},{3,131},{131,3},{4... | collective-permute-start | bytes 983048 | tf_op jit(solution)/shard_map/ppermute | solution.py:389
  11.3 16.9 %collective-permute-start = (bf16[128,1280]{1,0:T(8,128)(2,1)S(1)}, bf16[128,1280]{1,0:T(8,128)(2,1)S(1)}, u32[]{:S(2)}, u32[]{:S(2)}) collective-permute-start(bf16[128,1280]{1,0:T(8,128)(2,1)S(1)} %pad_maximum_fusion.4), channel_id=1, source_target_pairs={{0,0},{1,17},{2,34},{3,51},{4,68},{5,85},{6,102},{7,119},{8,8},{9,... | collective-permute-start | bytes 983048 | tf_op jit(solution)/shard_map/ppermute | solution.py:63
  30.2 30.2 %collective-permute-start.2 = (bf16[512,4096]{1,0:T(8,128)(2,1)}, bf16[512,4096]{1,0:T(8,128)(2,1)}, u32[]{:S(2)}, u32[]{:S(2)}) collective-permute-start(bf16[512,4096]{1,0:T(8,128)(2,1)} %bitcast.37), channel_id=1, source_target_pairs={{0,8},{8,0},{1,9},{9,1},{2,10},{10,2},{3,11},{11,3},{4,12},{12,4},... | collective-permute-start | bytes 12582920 | tf_op jit(solution)/shard_map/ppermute | solution.py:49
  30.9 11.6 %collective-permute-start.5 = (bf16[128,1280]{1,0:T(8,128)(2,1)S(1)}, bf16[128,1280]{1,0:T(8,128)(2,1)S(1)}, u32[]{:S(2)}, u32[]{:S(2)}) collective-permute-start(bf16[128,1280]{1,0:T(8,128)(2,1)S(1)} %collective-permute-done), channel_id=1, source_target_pairs={{0,129},{1,128},{2,131},{3,130},{4,133},{5,132},{6,135},{7,134},{8... | collective-permute-start | bytes 983048 | tf_op jit(solution)/shard_map/ppermute | solution.py:39
  32.1 15.4 %collective-permute-start.6 = (bf16[128,1280]{1,0:T(8,128)(2,1)S(1)}, bf16[128,1280]{1,0:T(8,128)(2,1)S(1)}, u32[]{:S(2)}, u32[]{:S(2)}) collective-permute-start(bf16[128,1280]{1,0:T(8,128)(2,1)S(1)} %collective-permute-done), channel_id=1, source_target_pairs={{0,1},{1,0},{2,3},{3,2},{4,5},{5,4},{6,7},{7,6},{8,12},{9,13},{10,... | collective-permute-start | bytes 983048 | tf_op jit(solution)/shard_map/ppermute | solution.py:39
  38.8 8.8 %collective-permute-start.4 = (bf16[128,1280]{1,0:T(8,128)(2,1)S(1)}, bf16[128,1280]{1,0:T(8,128)(2,1)S(1)}, u32[]{:S(2)}, u32[]{:S(2)}) collective-permute-start(bf16[128,1280]{1,0:T(8,128)(2,1)S(1)} %collective-permute-done), channel_id=1, source_target_pairs={{0,128},{1,129},{2,130},{3,131},{4,132},{5,133},{6,134},{7,135},{8... | collective-permute-start | bytes 983048 | tf_op jit(solution)/shard_map/ppermute | solution.py:39
  47.5 10.7 %collective-permute-start.8 = (bf16[2,128,1280]{2,1,0:T(8,128)(2,1)S(1)}, bf16[2,128,1280]{2,1,0:T(8,128)(2,1)S(1)}, u32[]{:S(2)}, u32[]{:S(2)}) collective-permute-start(bf16[2,128,1280]{2,1,0:T(8,128)(2,1)S(1)} %pad_maximum_fusion.2.refs_1_), channel_id=1, source_target_pairs={{0,6},{1,7},{2,0},{3,1},{4,2},{5,3},{6,4},{7,5},{8,137},{9,136},{1... | collective-permute-start | bytes 1966088 | tf_op jit(solution)/shard_map/ppermute | solution.py:39
  47.7 10.7 %collective-permute-start.7 = (bf16[2,128,1280]{2,1,0:T(8,128)(2,1)S(1)}, bf16[2,128,1280]{2,1,0:T(8,128)(2,1)S(1)}, u32[]{:S(2)}, u32[]{:S(2)}) collective-permute-start(bf16[2,128,1280]{2,1,0:T(8,128)(2,1)S(1)} %pad_maximum_fusion.1.refs_0_), channel_id=1, source_target_pairs={{0,2},{1,3},{2,4},{3,5},{4,6},{5,7},{6,0},{7,1},{8,136},{9,137},{1... | collective-permute-start | bytes 1966088 | tf_op jit(solution)/shard_map/ppermute | solution.py:39
  49.8 16.8 %collective-permute-start.10 = (bf16[2,128,1280]{2,1,0:T(8,128)(2,1)S(1)}, bf16[2,128,1280]{2,1,0:T(8,128)(2,1)S(1)}, u32[]{:S(2)}, u32[]{:S(2)}) collective-permute-start(bf16[2,128,1280]{2,1,0:T(8,128)(2,1)S(1)} %pad_maximum_fusion.2.refs_1_), channel_id=1, source_target_pairs={{0,2},{1,3},{2,4},{3,5},{4,6},{5,7},{6,0},{7,1},{8,136},{9,137},{1... | collective-permute-start | bytes 1966088 | tf_op jit(solution)/shard_map/ppermute | solution.py:39
  49.9 16.7 %collective-permute-start.9 = (bf16[2,128,1280]{2,1,0:T(8,128)(2,1)S(1)}, bf16[2,128,1280]{2,1,0:T(8,128)(2,1)}, u32[]{:S(2)}, u32[]{:S(2)}) collective-permute-start(bf16[2,128,1280]{2,1,0:T(8,128)(2,1)S(1)} %pad_maximum_fusion.1.refs_0_), channel_id=1, source_target_pairs={{0,6},{1,7},{2,0},{3,1},{4,2},{5,3},{6,4},{7,5},{8,137},{9,136},{1... | collective-permute-start | bytes 1966088 | tf_op jit(solution)/shard_map/ppermute | solution.py:39
  58.2 14.1 %collective-permute-start.12 = (bf16[2,128,1280]{2,1,0:T(8,128)(2,1)S(1)}, bf16[2,128,1280]{2,1,0:T(8,128)(2,1)}, u32[]{:S(2)}, u32[]{:S(2)}) collective-permute-start(bf16[2,128,1280]{2,1,0:T(8,128)(2,1)S(1)} %collective-permute-done.8.refs_3_), channel_id=1, source_target_pairs={{0,6},{1,7},{2,0},{3,1},{4,2},{5,3},{6,4},{7,5},{8,137},{9,136},{1... | collective-permute-start | bytes 1966088 | tf_op jit(solution)/shard_map/ppermute | solution.py:39
  58.4 14.1 %collective-permute-start.11 = (bf16[2,128,1280]{2,1,0:T(8,128)(2,1)S(1)}, bf16[2,128,1280]{2,1,0:T(8,128)(2,1)}, u32[]{:S(2)}, u32[]{:S(2)}) collective-permute-start(bf16[2,128,1280]{2,1,0:T(8,128)(2,1)S(1)} %collective-permute-done.7.refs_2_), channel_id=1, source_target_pairs={{0,2},{1,3},{2,4},{3,5},{4,6},{5,7},{6,0},{7,1},{8,136},{9,137},{1... | collective-permute-start | bytes 1966088 | tf_op jit(solution)/shard_map/ppermute | solution.py:39
  60.5 6.2 %collective-permute-start.3 = (f32[8,512]{1,0:T(8,128)S(1)}, f32[8,512]{1,0:T(8,128)S(1)}, u32[]{:S(2)}, u32[]{:S(2)}) collective-permute-start(f32[8,512]{1,0:T(8,128)S(1)} %bitcast.43), channel_id=1, source_target_pairs={{0,8},{8,0},{1,9},{9,1},{2,10},{10,2},{3,11},{11,3},{4,12},{12,4},... | collective-permute-start | bytes 49160 | tf_op jit(solution)/shard_map/ppermute | solution.py:49
  60.8 2.3 %copy-start = (bf16[1,512,4096]{2,1,0:T(8,128)(2,1)S(1)}, bf16[1,512,4096]{2,1,0:T(8,128)(2,1)}, u32[]{:S(2)}) copy-start(bf16[1,512,4096]{2,1,0:T(8,128)(2,1)} %param.9) | copy-start | bytes 12582916
  66.6 38.3 %copy-start.7 = (bf16[1,512,2,2]{1,3,2,0:T(2,128)(2,1)S(1)}, bf16[1,512,2,2]{1,3,2,0:T(2,128)(2,1)}, u32[]{:S(2)}) copy-start(bf16[1,512,2,2]{1,3,2,0:T(2,128)(2,1)} %param.17) | copy-start | bytes 12292
  66.6 38.3 %copy-start.4 = (s32[1,512,2,2]{1,3,2,0:T(2,128)S(1)}, s32[1,512,2,2]{1,3,2,0:T(2,128)}, u32[]{:S(2)}) copy-start(s32[1,512,2,2]{1,3,2,0:T(2,128)} %param.16) | copy-start | bytes 24580
  79.8 2.7 %collective-permute-start.13 = (f32[512,512]{1,0:T(8,128)S(1)}, f32[512,512]{1,0:T(8,128)S(1)}, u32[]{:S(2)}, u32[]{:S(2)}) collective-permute-start(f32[512,512]{1,0:T(8,128)S(1)} %get-tuple-element.15), channel_id=1, source_target_pairs={{0,8},{8,0},{1,9},{9,1},{2,10},{10,2},{3,11},{11,3},{4,12},{12,4},... | collective-permute-start | bytes 3145736 | tf_op jit(solution)/shard_map/ppermute | solution.py:49
  82.8 15.6 %collective-permute-start.14 = (bf16[512,512]{1,0:T(8,128)(2,1)S(1)}, bf16[512,512]{1,0:T(8,128)(2,1)S(1)}, u32[]{:S(2)}, u32[]{:S(2)}) collective-permute-start(bf16[512,512]{1,0:T(8,128)(2,1)S(1)} %add_convert_fusion.refs_0_), channel_id=1, source_target_pairs={{0,1},{1,0},{2,3},{3,2},{4,5},{5,4},{6,7},{7,6},{8,9},{9,8},{10,11... | collective-permute-start | bytes 1572872 | tf_op jit(solution)/shard_map/ppermute | solution.py:400
  85.3 18.2 %collective-permute-start.16 = (bf16[512,512]{1,0:T(8,128)(2,1)S(1)}, bf16[512,512]{1,0:T(8,128)(2,1)S(1)}, u32[]{:S(2)}, u32[]{:S(2)}) collective-permute-start(bf16[512,512]{1,0:T(8,128)(2,1)S(1)} %add_convert_fusion.refs_0_), channel_id=1, source_target_pairs={{0,4},{2,6},{1,5},{3,7},{8,12},{10,14},{9,13},{11,15},{16,20},{18,... | collective-permute-start | bytes 1572872 | tf_op jit(solution)/shard_map/ppermute | solution.py:403
  86.6 27.1 %collective-permute-start.15 = (bf16[512,512]{1,0:T(8,128)(2,1)S(1)}, bf16[512,512]{1,0:T(8,128)(2,1)S(1)}, u32[]{:S(2)}, u32[]{:S(2)}) collective-permute-start(bf16[512,512]{1,0:T(8,128)(2,1)S(1)} %add_convert_fusion.refs_0_), channel_id=1, source_target_pairs={{0,2},{2,4},{4,6},{1,3},{3,5},{5,7},{8,10},{10,12},{12,14},{9,11},... | collective-permute-start | bytes 1572872 | tf_op jit(solution)/shard_map/ppermute | solution.py:401
  89.9 23.8 %collective-permute-start.17 = (bf16[512,512]{1,0:T(8,128)(2,1)S(1)}, bf16[512,512]{1,0:T(8,128)(2,1)}, u32[]{:S(2)}, u32[]{:S(2)}) collective-permute-start(bf16[512,512]{1,0:T(8,128)(2,1)S(1)} %add_convert_fusion.refs_0_), channel_id=1, source_target_pairs={{0,6},{1,7},{8,14},{9,15},{16,22},{17,23},{24,30},{25,31},{32,38},... | collective-permute-start | bytes 1572872 | tf_op jit(solution)/shard_map/ppermute | solution.py:402
  98.3 26.5 %collective-permute-start.18 = (bf16[512,512]{1,0:T(8,128)(2,1)S(1)}, bf16[512,512]{1,0:T(8,128)(2,1)S(1)}, u32[]{:S(2)}, u32[]{:S(2)}) collective-permute-start(bf16[512,512]{1,0:T(8,128)(2,1)S(1)} %collective-permute-done.14.refs_1_), channel_id=1, source_target_pairs={{0,2},{2,4},{4,6},{1,3},{3,5},{5,7},{8,10},{10,12},{12,14},{9,11},... | collective-permute-start | bytes 1572872 | tf_op jit(solution)/shard_map/ppermute | solution.py:404
  102.4 22.4 %collective-permute-start.20 = (bf16[512,512]{1,0:T(8,128)(2,1)S(1)}, bf16[512,512]{1,0:T(8,128)(2,1)S(1)}, u32[]{:S(2)}, u32[]{:S(2)}) collective-permute-start(bf16[512,512]{1,0:T(8,128)(2,1)S(1)} %collective-permute-done.14.refs_1_), channel_id=1, source_target_pairs={{0,6},{1,7},{8,14},{9,15},{16,22},{17,23},{24,30},{25,31},{32,38},... | collective-permute-start | bytes 1572872 | tf_op jit(solution)/shard_map/ppermute | solution.py:405
  103.5 21.3 %collective-permute-start.19 = (bf16[512,512]{1,0:T(8,128)(2,1)S(1)}, bf16[512,512]{1,0:T(8,128)(2,1)}, u32[]{:S(2)}, u32[]{:S(2)}) collective-permute-start(bf16[512,512]{1,0:T(8,128)(2,1)S(1)} %collective-permute-done.16.refs_3_), channel_id=1, source_target_pairs={{0,1},{1,0},{2,3},{3,2},{4,5},{5,4},{6,7},{7,6},{8,9},{9,8},{10,11... | collective-permute-start | bytes 1572872 | tf_op jit(solution)/shard_map/ppermute | solution.py:406
  105.0 2.2 %copy-start.1 = (bf16[1,512,4096]{2,1,0:T(8,128)(2,1)S(1)}, bf16[1,512,4096]{2,1,0:T(8,128)(2,1)}, u32[]{:S(2)}) copy-start(bf16[1,512,4096]{2,1,0:T(8,128)(2,1)} %param.9) | copy-start | bytes 12582916
  107.2 4.0 %copy-start.2 = (bf16[32,1280,128]{2,1,0:T(8,128)(2,1)S(1)}, bf16[32,1280,128]{2,1,0:T(8,128)(2,1)}, u32[]{:S(2)}) copy-start(bf16[32,1280,128]{2,1,0:T(8,128)(2,1)} %all-gather.3.cloned.1.call-done) | copy-start | bytes 31457284
  111.2 13.7 %copy-start.3 = (bf16[32,1280,128]{2,1,0:T(8,128)(2,1)S(1)}, bf16[32,1280,128]{2,1,0:T(8,128)(2,1)}, u32[]{:S(2)}) copy-start(bf16[32,1280,128]{2,1,0:T(8,128)(2,1)} %all-gather.3.cloned.1.call-done) | copy-start | bytes 31457284
Sparse Core Ops, SparseCore 0:
  30.3 69.1 all-gather.2

commit v3 on v2

--- a/solution.py
+++ b/solution.py
@@ -215,13 +215,14 @@
     for head in range(HEADS):
         lanes = slice(head * DH, (head + 1) * DH)
         one = slice(head, head + 1)
+        keys, mixed, shift = (kv[0], kv[1], 0) if isinstance(kv, tuple) else (kv, kv, WIDTH)
         scores = lax.dot_general(
-            kv[:, lanes],
+            keys[:, lanes],
             q_ref[:, lanes],
             (((1,), (1,)), ((), ())),
             preferred_element_type=jnp.float32,
         )
-        values = kv[:, WIDTH + head * DH : WIDTH + (head + 1) * DH]
+        values = mixed[:, shift + head * DH : shift + (head + 1) * DH]
         if diagonal:
             k_pos = lax.broadcasted_iota(jnp.int32, scores.shape, 0)
             q_pos = lax.broadcasted_iota(jnp.int32, scores.shape, 1)
@@ -265,7 +266,8 @@
 
 
 def attend_late_kernel(needs, place_ref, q_ref, m_in, l_in, acc_in, mix_ref, panels, *refs):
-    count = len(needs)
+    count = len(needs) + 1
+    blocks = ((refs[0], refs[1]),) + refs[2:count]
     out_hbm = refs[count]
     m_ref, l_ref, acc_ref, mixed_ref, w_ref, o_ref, w_sem, o_sem = refs[count + 1 :]
     depth = mixed_ref.shape[1]
@@ -284,7 +286,7 @@
     m_ref[...] = m_in[...]
     l_ref[...] = l_in[...]
     acc_ref[...] = acc_in[...]
-    attend_blocks(place_ref, needs, False, q_ref, refs[:count], m_ref, l_ref, acc_ref)
+    attend_blocks(place_ref, needs, False, q_ref, blocks, m_ref, l_ref, acc_ref)
     mix = jnp.transpose(mix_ref[...])
     for head in range(HEADS):
         attended = acc_ref[head * DH : (head + 1) * DH] / l_ref[head : head + 1]
@@ -401,7 +403,8 @@
     own_1 = lax.ppermute(own, "y", [(0, 1), (1, 2), (2, 3)])
     own_3 = lax.ppermute(own, "y", [(0, 3)])
     own_2 = lax.ppermute(own, "y", [(0, 2), (1, 3)])
-    other_1 = lax.ppermute(other, "y", [(0, 1), (1, 2), (2, 3)])
+    other_1k = lax.ppermute(other[:, :WIDTH], "y", [(0, 1), (1, 2), (2, 3)])
+    other_1v = lax.ppermute(own_1[:, WIDTH:], "x_hi", [(0, 1), (1, 0)])
     other_3 = lax.ppermute(other, "y", [(0, 3)])
     other_2 = lax.ppermute(own_2, "x_hi", [(0, 1), (1, 0)])
     state = attend_early(
@@ -413,7 +416,7 @@
         state,
         output_mix,
         panels,
-        [other_1, other_2, other_3],
+        [other_1k, other_1v, other_2, other_3],
         ((1, 0), (2, 0), (3, 0)),
     )
     return result[None]

time: 145 us -> 147 us (1.014); the launches traced: 142 us -> 147 us
  starting transfers between devices: 39.8 us -> 42 us
    ppermute x1, waiting for transfers between devices: 0.42 us -> 9.65 us  [on_device(): own_2 = lax.ppermute(own, 'y', [(0, 2), (1, 3)])]
    ppermute x1, waiting for transfers between devices: 6.92 us -> 0.01 us  [on_device(): other = lax.ppermute(own, 'x_hi', [(0, 1), (1, 0)])]
    ppermute x1 -> x2, waiting for transfers between devices: 4.79 us -> 0.01 us  [the longest x1 0.01 us: on_device(): other_1v = lax.ppermute(own_1[:, WIDTH:], 'x_hi', [(0, 1), (1, 0)])]
    ppermute x1, waiting for transfers between devices: 0.01 us -> 3.51 us  [on_device(): own_1 = lax.ppermute(own, 'y', [(0, 1), (1, 2), (2, 3)])]
    ppermute x1 -> x2, starting transfers between devices: 4.09 us -> 5.53 us  [the longest x1 3.27 us: on_device(): other_1k = lax.ppermute(other[:, :WIDTH], 'y', [(0, 1), (1, 2), (2, 3)])]
  transfers between devices with their start and end apart: 22 -> 23, of which waited for: 11 -> 10; matrix products, arithmetic and copies ran while one was open for 2% -> 3% of each run, Pallas kernels for 14% -> 13%
where the time goes in v3:
time: 147 us
  waiting for transfers between devices  45.1 us (31%)
  starting transfers between devices  42 us (29%)
  Pallas kernels  29.8 us (20%)
  between operations  13.7 us (9%)
  local copies, waits for them, and re-layouts  12.7 us (9%)
  other arithmetic  3.48 us (2%)
    ppermute x9, waiting for transfers between devices, moved(): return lax.ppermute(x, AXES, pairs)  20 us
    ppermute x9, starting transfers between devices, moved(): return lax.ppermute(x, AXES, pairs)  15.3 us
    unnamed x18, local copies, waits for them, and re-layouts  10.2 us
    pallas_call x1, Pallas kernels, attend_late(): pl.pallas_call(functools.partial(attend_late_kernel, needs), in_specs=[pl...  10.1 us
    ppermute x1, waiting for transfers between devices, on_device(): own_2 = lax.ppermute(own, 'y', [(0, 2), (1, 3)])  9.65 us
    ppermute x1, waiting for transfers between devices, lifted(): return lax.ppermute(x, AXES, pairs)  9.13 us
    ppermute x1, starting transfers between devices, lifted(): return lax.ppermute(x, AXES, pairs)  7.75 us
    pallas_call x1, Pallas kernels, project(): pl.pallas_call(functools.partial(project_kernel, count), in_specs=[pl.Blo...  7.43 us
  transfers between devices with their start and end apart: 23, of which 10 were waited for; matrix products, arithmetic and copies ran while one was open for 3% of the time, Pallas kernels for 13%

profile of v3, /device:TPU:54, one launch (start us, length us, event | category | flops | bytes accessed | tf_op | source)
XLA Modules:
  0.0 146.9 jit_solution(6081434407965632454)
XLA Ops:
  6.5 0.9 copy.24
  7.4 1.0 pad_maximum_fusion.3
  8.4 0.9 collective-permute-start.1
  9.3 1.1 reshape.38
  10.4 0.9 copy.27
  11.3 7.8 %collective-permute-start = (bf16[128,1280]{1,0:T(8,128)(2,1)S(1)}, bf16[128,1280]{1,0:T(8,128)(2,1)S(1)}, u32[]{:S(2)}, u32[]{:S(2)}) collective-permute-start(bf16[128,1280]{1,0:T(8,128)(2,1)S(1)} %pad_maximum_fusion.4), channel_id=1, source_target_pairs={{0,0},{1,17},{2,34},{3,51},{4,68},{5,85},{6,102},{7,119},{8,8},{9,... | collective-permute-start | bytes 983048 | tf_op jit(solution)/shard_map/ppermute | solution.py:63
  19.1 0.0 collective-permute-done.1
  19.1 9.1 %collective-permute-done = bf16[128,1280]{1,0:T(8,128)(2,1)S(1)} collective-permute-done((bf16[128,1280]{1,0:T(8,128)(2,1)S(1)}, bf16[128,1280]{1,0:T(8,128)(2,1)S(1)}, u32[]{:S(2)}, u32[]{:S(2)}) %collective-permute-start) | collective-permute-done | bytes 327712 | tf_op jit(solution)/shard_map/ppermute | solution.py:63
  28.2 1.1 select_bitcast_fusion.1
  29.3 0.9 pad_maximum_fusion
  30.2 0.0 all-gather.3.cloned.1.call-update
  30.2 0.7 collective-permute-start.2
  30.9 1.2 collective-permute-start.5
  32.1 6.8 %collective-permute-start.6 = (bf16[128,1280]{1,0:T(8,128)(2,1)S(1)}, bf16[128,1280]{1,0:T(8,128)(2,1)S(1)}, u32[]{:S(2)}, u32[]{:S(2)}) collective-permute-start(bf16[128,1280]{1,0:T(8,128)(2,1)S(1)} %collective-permute-done), channel_id=1, source_target_pairs={{0,1},{1,0},{2,3},{3,2},{4,5},{5,4},{6,7},{7,6},{8,12},{9,13},{10,... | collective-permute-start | bytes 983048 | tf_op jit(solution)/shard_map/ppermute | solution.py:39
  38.8 1.1 collective-permute-start.4
  40.0 2.5 %collective-permute-done.5 = bf16[128,1280]{1,0:T(8,128)(2,1)S(1)} collective-permute-done((bf16[128,1280]{1,0:T(8,128)(2,1)S(1)}, bf16[128,1280]{1,0:T(8,128)(2,1)S(1)}, u32[]{:S(2)}, u32[]{:S(2)}) %collective-permute-start.5) | collective-permute-done | bytes 327712 | tf_op jit(solution)/shard_map/ppermute | solution.py:39
  42.4 5.1 %collective-permute-done.6 = bf16[128,1280]{1,0:T(8,128)(2,1)S(1)} collective-permute-done((bf16[128,1280]{1,0:T(8,128)(2,1)S(1)}, bf16[128,1280]{1,0:T(8,128)(2,1)S(1)}, u32[]{:S(2)}, u32[]{:S(2)}) %collective-permute-start.6) | collective-permute-done | bytes 327712 | tf_op jit(solution)/shard_map/ppermute | solution.py:39
  47.5 0.1 pad_maximum_fusion.2.refs_1_
  47.5 0.1 collective-permute-start.8
  47.6 0.0 collective-permute-done.4
  47.7 0.1 pad_maximum_fusion.1.refs_0_
  47.7 2.1 %collective-permute-start.7 = (bf16[2,128,1280]{2,1,0:T(8,128)(2,1)S(1)}, bf16[2,128,1280]{2,1,0:T(8,128)(2,1)S(1)}, u32[]{:S(2)}, u32[]{:S(2)}) collective-permute-start(bf16[2,128,1280]{2,1,0:T(8,128)(2,1)S(1)} %pad_maximum_fusion.1.refs_0_), channel_id=1, source_target_pairs={{0,2},{1,3},{2,4},{3,5},{4,6},{5,7},{6,0},{7,1},{8,136},{9,137},{1... | collective-permute-start | bytes 1966088 | tf_op jit(solution)/shard_map/ppermute | solution.py:39
  49.8 0.1 collective-permute-start.10
  49.9 1.9 %collective-permute-start.9 = (bf16[2,128,1280]{2,1,0:T(8,128)(2,1)S(1)}, bf16[2,128,1280]{2,1,0:T(8,128)(2,1)}, u32[]{:S(2)}, u32[]{:S(2)}) collective-permute-start(bf16[2,128,1280]{2,1,0:T(8,128)(2,1)S(1)} %pad_maximum_fusion.1.refs_0_), channel_id=1, source_target_pairs={{0,6},{1,7},{2,0},{3,1},{4,2},{5,3},{6,4},{7,5},{8,137},{9,136},{1... | collective-permute-start | bytes 1966088 | tf_op jit(solution)/shard_map/ppermute | solution.py:39
  51.8 6.4 %collective-permute-done.8.refs_3_ = bf16[2,128,1280]{2,1,0:T(8,128)(2,1)S(1)} collective-permute-done((bf16[2,128,1280]{2,1,0:T(8,128)(2,1)S(1)}, bf16[2,128,1280]{2,1,0:T(8,128)(2,1)S(1)}, u32[]{:S(2)}, u32[]{:S(2)}) %collective-permute-start.8) | collective-permute-done | bytes 655392 | tf_op jit(solution)/shard_map/ppermute | solution.py:39
  58.2 0.0 collective-permute-start.12
  58.2 0.2 collective-permute-done.7.refs_2_
  58.4 2.0 %collective-permute-start.11 = (bf16[2,128,1280]{2,1,0:T(8,128)(2,1)S(1)}, bf16[2,128,1280]{2,1,0:T(8,128)(2,1)}, u32[]{:S(2)}, u32[]{:S(2)}) collective-permute-start(bf16[2,128,1280]{2,1,0:T(8,128)(2,1)S(1)} %collective-permute-done.7.refs_2_), channel_id=1, source_target_pairs={{0,2},{1,3},{2,4},{3,5},{4,6},{5,7},{6,0},{7,1},{8,136},{9,137},{1... | collective-permute-start | bytes 1966088 | tf_op jit(solution)/shard_map/ppermute | solution.py:39
  60.5 0.3 collective-permute-start.3
  60.7 0.1 pad_add_fusion.place_ref
  60.8 2.3 %copy-done = bf16[1,512,4096]{2,1,0:T(8,128)(2,1)S(1)} copy-done((bf16[1,512,4096]{2,1,0:T(8,128)(2,1)S(1)}, bf16[1,512,4096]{2,1,0:T(8,128)(2,1)}, u32[]{:S(2)}) %copy-start) | copy-done | bytes 4194328
  63.1 3.5 %shard_map.92.x_ref = bf16[1024,2048]{1,0:T(8,128)(2,1)S(1)} custom-call(s32[4]{0:T(128)S(1)} %pad_add_fusion.place_ref, bf16[512,4096]{1,0:T(8,128)(2,1)S(1)} %bitcast.38, bf16[512,4096]{1,0:T(8,128)(2,1)} %collective-permute-done.2.other_ref), custom_call_target="tpu_custom_call" | custom-call | bytes 12582912 | tf_op jit(solution)/shard_map/pallas_call | solution.py:102
  66.6 0.0 copy-start.7
  66.6 0.0 copy-start.4
  66.6 0.0 collective-permute-done.3.far_mix_ref
  66.6 0.0 collective-permute-done.10.refs_5_
  66.6 5.7 %collective-permute-done.12.refs_7_ = bf16[2,128,1280]{2,1,0:T(8,128)(2,1)} collective-permute-done((bf16[2,128,1280]{2,1,0:T(8,128)(2,1)S(1)}, bf16[2,128,1280]{2,1,0:T(8,128)(2,1)}, u32[]{:S(2)}, u32[]{:S(2)}) %collective-permute-start.12) | collective-permute-done | bytes 655392 | tf_op jit(solution)/shard_map/ppermute | solution.py:39
  72.4 0.2 collective-permute-done.11.refs_6_
  72.5 7.4 %shard_map.93 = (f32[512,512]{1,0:T(8,128)S(1)}, f32[512,512]{1,0:T(8,128)S(1)}) custom-call(s32[4]{0:T(128)S(1)} %pad_add_fusion.place_ref, bf16[1024,2048]{1,0:T(8,128)(2,1)S(1)} %shard_map.92.x_ref, f32[8,512]{1,0:T(8,128)S(1)} %bitcast.44, f32[8,512]{1,0:T(8,128)S(1)} %collective-permute-done.3.far_mix_ref, ...), custom_call_target="tpu_custom_call" | custom-call | flops 5368709120 | bytes 9437184 | tf_op jit(solution)/shard_map/pallas_call | solution.py:147
  80.0 0.1 collective-permute-start.13
  80.1 2.8 %collective-permute-done.13 = f32[512,512]{1,0:T(8,128)S(1)} collective-permute-done((f32[512,512]{1,0:T(8,128)S(1)}, f32[512,512]{1,0:T(8,128)S(1)}, u32[]{:S(2)}, u32[]{:S(2)}) %collective-permute-start.13) | collective-permute-done | bytes 1048608 | tf_op jit(solution)/shard_map/ppermute | solution.py:49
  82.8 0.3 add_convert_fusion.refs_0_
  83.1 1.3 collective-permute-start.16
  84.4 2.3 %collective-permute-start.14 = (bf16[512,512]{1,0:T(8,128)(2,1)S(1)}, bf16[512,512]{1,0:T(8,128)(2,1)S(1)}, u32[]{:S(2)}, u32[]{:S(2)}) collective-permute-start(bf16[512,512]{1,0:T(8,128)(2,1)S(1)} %add_convert_fusion.refs_0_), channel_id=1, source_target_pairs={{0,1},{1,0},{2,3},{3,2},{4,5},{5,4},{6,7},{7,6},{8,9},{9,8},{10,11... | collective-permute-start | bytes 1572872 | tf_op jit(solution)/shard_map/ppermute | solution.py:402
  86.7 3.4 %collective-permute-start.15 = (bf16[512,512]{1,0:T(8,128)(2,1)S(1)}, bf16[512,512]{1,0:T(8,128)(2,1)S(1)}, u32[]{:S(2)}, u32[]{:S(2)}) collective-permute-start(bf16[512,512]{1,0:T(8,128)(2,1)S(1)} %add_convert_fusion.refs_0_), channel_id=1, source_target_pairs={{0,2},{2,4},{4,6},{1,3},{3,5},{5,7},{8,10},{10,12},{12,14},{9,11},... | collective-permute-start | bytes 1572872 | tf_op jit(solution)/shard_map/ppermute | solution.py:403
  90.2 1.5 %collective-permute-start.17 = (bf16[512,512]{1,0:T(8,128)(2,1)S(1)}, bf16[512,512]{1,0:T(8,128)(2,1)}, u32[]{:S(2)}, u32[]{:S(2)}) collective-permute-start(bf16[512,512]{1,0:T(8,128)(2,1)S(1)} %add_convert_fusion.refs_0_), channel_id=1, source_target_pairs={{0,6},{1,7},{8,14},{9,15},{16,22},{17,23},{24,30},{25,31},{32,38},... | collective-permute-start | bytes 1572872 | tf_op jit(solution)/shard_map/ppermute | solution.py:404
  91.6 9.6 %collective-permute-done.16.refs_3_ = bf16[512,512]{1,0:T(8,128)(2,1)S(1)} collective-permute-done((bf16[512,512]{1,0:T(8,128)(2,1)S(1)}, bf16[512,512]{1,0:T(8,128)(2,1)S(1)}, u32[]{:S(2)}, u32[]{:S(2)}) %collective-permute-start.16) | collective-permute-done | bytes 524320 | tf_op jit(solution)/shard_map/ppermute | solution.py:405
  101.3 2.3 %collective-permute-start.20 = (bf16[512,512]{1,0:T(8,128)(2,1)S(1)}, bf16[512,512]{1,0:T(8,128)(2,1)S(1)}, u32[]{:S(2)}, u32[]{:S(2)}) collective-permute-start(bf16[512,512]{1,0:T(8,128)(2,1)S(1)} %collective-permute-done.16.refs_3_), channel_id=1, source_target_pairs={{0,1},{1,0},{2,3},{3,2},{4,5},{5,4},{6,7},{7,6},{8,9},{9,8},{10,11... | collective-permute-start | bytes 1572872 | tf_op jit(solution)/shard_map/ppermute | solution.py:409
  103.6 0.0 collective-permute-done.14.refs_1_
  103.6 0.7 collective-permute-start.21
  104.3 0.7 slice.8
  105.0 3.3 %collective-permute-start.18 = (bf16[512,256]{1,0:T(8,128)(2,1)}, bf16[512,256]{1,0:T(8,128)(2,1)S(1)}, u32[]{:S(2)}, u32[]{:S(2)}) collective-permute-start(bf16[512,256]{1,0:T(8,128)(2,1)} %slice.8), channel_id=1, source_target_pairs={{0,2},{2,4},{4,6},{1,3},{3,5},{5,7},{8,10},{10,12},{12,14},{9,11},... | collective-permute-start | bytes 786440 | tf_op jit(solution)/shard_map/ppermute | solution.py:406
  108.3 3.5 %collective-permute-done.15.refs_2_ = bf16[512,512]{1,0:T(8,128)(2,1)S(1)} collective-permute-done((bf16[512,512]{1,0:T(8,128)(2,1)S(1)}, bf16[512,512]{1,0:T(8,128)(2,1)S(1)}, u32[]{:S(2)}, u32[]{:S(2)}) %collective-permute-start.15) | collective-permute-done | bytes 524320 | tf_op jit(solution)/shard_map/ppermute | solution.py:403
  111.8 0.7 slice.9
  112.5 2.3 %collective-permute-start.19 = (bf16[512,256]{1,0:T(8,128)(2,1)}, bf16[512,256]{1,0:T(8,128)(2,1)}, u32[]{:S(2)}, u32[]{:S(2)}) collective-permute-start(bf16[512,256]{1,0:T(8,128)(2,1)} %slice.9), channel_id=1, source_target_pairs={{0,1},{1,0},{2,3},{3,2},{4,5},{5,4},{6,7},{7,6},{8,9},{9,8},{10,11... | collective-permute-start | bytes 786440 | tf_op jit(solution)/shard_map/ppermute | solution.py:407
  114.8 0.0 all-gather.3.cloned.1.call-done
  114.8 0.0 copy-start.1
  114.8 2.2 %copy-done.1 = bf16[1,512,4096]{2,1,0:T(8,128)(2,1)S(1)} copy-done((bf16[1,512,4096]{2,1,0:T(8,128)(2,1)S(1)}, bf16[1,512,4096]{2,1,0:T(8,128)(2,1)}, u32[]{:S(2)}) %copy-start.1) | copy-done | bytes 4194328
  117.0 4.0 %copy-done.2 = bf16[32,1280,128]{2,1,0:T(8,128)(2,1)S(1)} copy-done((bf16[32,1280,128]{2,1,0:T(8,128)(2,1)S(1)}, bf16[32,1280,128]{2,1,0:T(8,128)(2,1)}, u32[]{:S(2)}) %copy-start.2) | copy-done | bytes 10485784
  121.0 2.5 %shard_map.91.q_ref = bf16[512,256]{1,0:T(8,128)(2,1)S(1)} custom-call(bf16[512,4096]{1,0:T(8,128)(2,1)S(1)} %bitcast.39, bf16[16,2,1280,128]{3,2,1,0:T(8,128)(2,1)S(1)} %bitcast.40), custom_call_target="tpu_custom_call" | custom-call | flops 1073741824 | bytes 6291456 | tf_op jit(solution)/shard_map/pallas_call | solution.py:190
  123.5 6.3 %shard_map.94 = (f32[2,512]{1,0:T(2,128)S(1)}, f32[2,512]{1,0:T(2,128)S(1)}, f32[256,512]{1,0:T(8,128)S(1)}) custom-call(s32[4]{0:T(128)S(1)} %pad_add_fusion.place_ref, bf16[512,256]{1,0:T(8,128)(2,1)S(1)} %shard_map.91.q_ref, bf16[512,512]{1,0:T(8,128)(2,1)S(1)} %add_convert_fusion.refs_0_, bf16[512,512]{1,0:T(8,128)(2,1)S(1)} %collective-permute-done.14.refs_1_, ...), custom_call_target="tpu_custom_call" | custom-call | flops 1342177280 | bytes 2621440 | tf_op jit(solution)/shard_map/pallas_call | solution.py:332
  129.9 0.0 collective-permute-done.19.refs_1_
  129.9 0.0 collective-permute-done.20.refs_2_
  129.9 10.1 %shard_map.95 = bf16[512,4096]{1,0:T(8,128)(2,1)} custom-call(s32[4]{0:T(128)S(1)} %pad_add_fusion.place_ref, bf16[512,256]{1,0:T(8,128)(2,1)S(1)} %shard_map.91.q_ref, f32[2,512]{1,0:T(2,128)S(1)} %get-tuple-element.16.m_in, f32[2,512]{1,0:T(2,128)S(1)} %get-tuple-element.17.l_in, f32[256,512]{1,0:T(8,128)S(1)} %get-tuple-element.18.acc_in, ...), custom_call_target="tpu_custom_call" | custom-call | flops 5368709120 | bytes 2097152 | tf_op jit(solution)/shard_map/pallas_call | solution.py:349
  (23 shorter events, 0.1 us)
Async XLA Ops:
  6.5 53.9 %copy-start.6 = (bf16[1,512,2,2]{1,3,2,0:T(2,128)(2,1)S(1)}, bf16[1,512,2,2]{1,3,2,0:T(2,128)(2,1)}, u32[]{:S(2)}) copy-start(bf16[1,512,2,2]{1,3,2,0:T(2,128)(2,1)} %param.15) | copy-start | bytes 12292
  6.5 53.9 %copy-start.5 = (s32[1,512,2,2]{1,3,2,0:T(2,128)S(1)}, s32[1,512,2,2]{1,3,2,0:T(2,128)}, u32[]{:S(2)}) copy-start(s32[1,512,2,2]{1,3,2,0:T(2,128)} %param.14) | copy-start | bytes 24580
  6.5 108.3 %all-gather.3.cloned.1.call-start = ((), (), s32[]{:S(2)}) async-start(), calls=%async_computation | async-start | bytes 11141120 | tf_op jit(solution)/shard_map/all_gather | solution.py:397
  8.4 10.7 %collective-permute-start.1 = (bf16[1280,128]{1,0:T(8,128)(2,1)S(1)}, bf16[1280,128]{1,0:T(8,128)(2,1)S(1)}, u32[]{:S(2)}, u32[]{:S(2)}) collective-permute-start(bf16[1280,128]{1,0:T(8,128)(2,1)S(1)} %pad_maximum_fusion.3), channel_id=1, source_target_pairs={{0,128},{128,0},{1,129},{129,1},{2,130},{130,2},{3,131},{131,3},{4... | collective-permute-start | bytes 983048 | tf_op jit(solution)/shard_map/ppermute | solution.py:391
  11.3 16.9 %collective-permute-start = (bf16[128,1280]{1,0:T(8,128)(2,1)S(1)}, bf16[128,1280]{1,0:T(8,128)(2,1)S(1)}, u32[]{:S(2)}, u32[]{:S(2)}) collective-permute-start(bf16[128,1280]{1,0:T(8,128)(2,1)S(1)} %pad_maximum_fusion.4), channel_id=1, source_target_pairs={{0,0},{1,17},{2,34},{3,51},{4,68},{5,85},{6,102},{7,119},{8,8},{9,... | collective-permute-start | bytes 983048 | tf_op jit(solution)/shard_map/ppermute | solution.py:63
  30.2 30.2 %collective-permute-start.2 = (bf16[512,4096]{1,0:T(8,128)(2,1)}, bf16[512,4096]{1,0:T(8,128)(2,1)}, u32[]{:S(2)}, u32[]{:S(2)}) collective-permute-start(bf16[512,4096]{1,0:T(8,128)(2,1)} %bitcast.37), channel_id=1, source_target_pairs={{0,8},{8,0},{1,9},{9,1},{2,10},{10,2},{3,11},{11,3},{4,12},{12,4},... | collective-permute-start | bytes 12582920 | tf_op jit(solution)/shard_map/ppermute | solution.py:49
  30.9 11.6 %collective-permute-start.5 = (bf16[128,1280]{1,0:T(8,128)(2,1)S(1)}, bf16[128,1280]{1,0:T(8,128)(2,1)S(1)}, u32[]{:S(2)}, u32[]{:S(2)}) collective-permute-start(bf16[128,1280]{1,0:T(8,128)(2,1)S(1)} %collective-permute-done), channel_id=1, source_target_pairs={{0,129},{1,128},{2,131},{3,130},{4,133},{5,132},{6,135},{7,134},{8... | collective-permute-start | bytes 983048 | tf_op jit(solution)/shard_map/ppermute | solution.py:39
  32.1 15.4 %collective-permute-start.6 = (bf16[128,1280]{1,0:T(8,128)(2,1)S(1)}, bf16[128,1280]{1,0:T(8,128)(2,1)S(1)}, u32[]{:S(2)}, u32[]{:S(2)}) collective-permute-start(bf16[128,1280]{1,0:T(8,128)(2,1)S(1)} %collective-permute-done), channel_id=1, source_target_pairs={{0,1},{1,0},{2,3},{3,2},{4,5},{5,4},{6,7},{7,6},{8,12},{9,13},{10,... | collective-permute-start | bytes 983048 | tf_op jit(solution)/shard_map/ppermute | solution.py:39
  38.8 8.8 %collective-permute-start.4 = (bf16[128,1280]{1,0:T(8,128)(2,1)S(1)}, bf16[128,1280]{1,0:T(8,128)(2,1)S(1)}, u32[]{:S(2)}, u32[]{:S(2)}) collective-permute-start(bf16[128,1280]{1,0:T(8,128)(2,1)S(1)} %collective-permute-done), channel_id=1, source_target_pairs={{0,128},{1,129},{2,130},{3,131},{4,132},{5,133},{6,134},{7,135},{8... | collective-permute-start | bytes 983048 | tf_op jit(solution)/shard_map/ppermute | solution.py:39
  47.5 10.7 %collective-permute-start.8 = (bf16[2,128,1280]{2,1,0:T(8,128)(2,1)S(1)}, bf16[2,128,1280]{2,1,0:T(8,128)(2,1)S(1)}, u32[]{:S(2)}, u32[]{:S(2)}) collective-permute-start(bf16[2,128,1280]{2,1,0:T(8,128)(2,1)S(1)} %pad_maximum_fusion.2.refs_1_), channel_id=1, source_target_pairs={{0,6},{1,7},{2,0},{3,1},{4,2},{5,3},{6,4},{7,5},{8,137},{9,136},{1... | collective-permute-start | bytes 1966088 | tf_op jit(solution)/shard_map/ppermute | solution.py:39
  47.7 10.7 %collective-permute-start.7 = (bf16[2,128,1280]{2,1,0:T(8,128)(2,1)S(1)}, bf16[2,128,1280]{2,1,0:T(8,128)(2,1)S(1)}, u32[]{:S(2)}, u32[]{:S(2)}) collective-permute-start(bf16[2,128,1280]{2,1,0:T(8,128)(2,1)S(1)} %pad_maximum_fusion.1.refs_0_), channel_id=1, source_target_pairs={{0,2},{1,3},{2,4},{3,5},{4,6},{5,7},{6,0},{7,1},{8,136},{9,137},{1... | collective-permute-start | bytes 1966088 | tf_op jit(solution)/shard_map/ppermute | solution.py:39
  49.8 16.8 %collective-permute-start.10 = (bf16[2,128,1280]{2,1,0:T(8,128)(2,1)S(1)}, bf16[2,128,1280]{2,1,0:T(8,128)(2,1)}, u32[]{:S(2)}, u32[]{:S(2)}) collective-permute-start(bf16[2,128,1280]{2,1,0:T(8,128)(2,1)S(1)} %pad_maximum_fusion.2.refs_1_), channel_id=1, source_target_pairs={{0,2},{1,3},{2,4},{3,5},{4,6},{5,7},{6,0},{7,1},{8,136},{9,137},{1... | collective-permute-start | bytes 1966088 | tf_op jit(solution)/shard_map/ppermute | solution.py:39
  49.9 16.7 %collective-permute-start.9 = (bf16[2,128,1280]{2,1,0:T(8,128)(2,1)S(1)}, bf16[2,128,1280]{2,1,0:T(8,128)(2,1)}, u32[]{:S(2)}, u32[]{:S(2)}) collective-permute-start(bf16[2,128,1280]{2,1,0:T(8,128)(2,1)S(1)} %pad_maximum_fusion.1.refs_0_), channel_id=1, source_target_pairs={{0,6},{1,7},{2,0},{3,1},{4,2},{5,3},{6,4},{7,5},{8,137},{9,136},{1... | collective-permute-start | bytes 1966088 | tf_op jit(solution)/shard_map/ppermute | solution.py:39
  58.2 14.1 %collective-permute-start.12 = (bf16[2,128,1280]{2,1,0:T(8,128)(2,1)S(1)}, bf16[2,128,1280]{2,1,0:T(8,128)(2,1)}, u32[]{:S(2)}, u32[]{:S(2)}) collective-permute-start(bf16[2,128,1280]{2,1,0:T(8,128)(2,1)S(1)} %collective-permute-done.8.refs_3_), channel_id=1, source_target_pairs={{0,6},{1,7},{2,0},{3,1},{4,2},{5,3},{6,4},{7,5},{8,137},{9,136},{1... | collective-permute-start | bytes 1966088 | tf_op jit(solution)/shard_map/ppermute | solution.py:39
  58.4 14.1 %collective-permute-start.11 = (bf16[2,128,1280]{2,1,0:T(8,128)(2,1)S(1)}, bf16[2,128,1280]{2,1,0:T(8,128)(2,1)}, u32[]{:S(2)}, u32[]{:S(2)}) collective-permute-start(bf16[2,128,1280]{2,1,0:T(8,128)(2,1)S(1)} %collective-permute-done.7.refs_2_), channel_id=1, source_target_pairs={{0,2},{1,3},{2,4},{3,5},{4,6},{5,7},{6,0},{7,1},{8,136},{9,137},{1... | collective-permute-start | bytes 1966088 | tf_op jit(solution)/shard_map/ppermute | solution.py:39
  60.5 6.2 %collective-permute-start.3 = (f32[8,512]{1,0:T(8,128)S(1)}, f32[8,512]{1,0:T(8,128)S(1)}, u32[]{:S(2)}, u32[]{:S(2)}) collective-permute-start(f32[8,512]{1,0:T(8,128)S(1)} %bitcast.43), channel_id=1, source_target_pairs={{0,8},{8,0},{1,9},{9,1},{2,10},{10,2},{3,11},{11,3},{4,12},{12,4},... | collective-permute-start | bytes 49160 | tf_op jit(solution)/shard_map/ppermute | solution.py:49
  60.8 2.3 %copy-start = (bf16[1,512,4096]{2,1,0:T(8,128)(2,1)S(1)}, bf16[1,512,4096]{2,1,0:T(8,128)(2,1)}, u32[]{:S(2)}) copy-start(bf16[1,512,4096]{2,1,0:T(8,128)(2,1)} %param.9) | copy-start | bytes 12582916
  66.6 37.7 %copy-start.7 = (bf16[1,512,2,2]{1,3,2,0:T(2,128)(2,1)S(1)}, bf16[1,512,2,2]{1,3,2,0:T(2,128)(2,1)}, u32[]{:S(2)}) copy-start(bf16[1,512,2,2]{1,3,2,0:T(2,128)(2,1)} %param.17) | copy-start | bytes 12292
  66.6 48.2 %copy-start.4 = (s32[1,512,2,2]{1,3,2,0:T(2,128)S(1)}, s32[1,512,2,2]{1,3,2,0:T(2,128)}, u32[]{:S(2)}) copy-start(s32[1,512,2,2]{1,3,2,0:T(2,128)} %param.16) | copy-start | bytes 24580
  80.0 2.9 %collective-permute-start.13 = (f32[512,512]{1,0:T(8,128)S(1)}, f32[512,512]{1,0:T(8,128)S(1)}, u32[]{:S(2)}, u32[]{:S(2)}) collective-permute-start(f32[512,512]{1,0:T(8,128)S(1)} %get-tuple-element.15), channel_id=1, source_target_pairs={{0,8},{8,0},{1,9},{9,1},{2,10},{10,2},{3,11},{11,3},{4,12},{12,4},... | collective-permute-start | bytes 3145736 | tf_op jit(solution)/shard_map/ppermute | solution.py:49
  83.1 18.2 %collective-permute-start.16 = (bf16[512,512]{1,0:T(8,128)(2,1)S(1)}, bf16[512,512]{1,0:T(8,128)(2,1)S(1)}, u32[]{:S(2)}, u32[]{:S(2)}) collective-permute-start(bf16[512,512]{1,0:T(8,128)(2,1)S(1)} %add_convert_fusion.refs_0_), channel_id=1, source_target_pairs={{0,4},{2,6},{1,5},{3,7},{8,12},{10,14},{9,13},{11,15},{16,20},{18,... | collective-permute-start | bytes 1572872 | tf_op jit(solution)/shard_map/ppermute | solution.py:405
  84.4 19.2 %collective-permute-start.14 = (bf16[512,512]{1,0:T(8,128)(2,1)S(1)}, bf16[512,512]{1,0:T(8,128)(2,1)S(1)}, u32[]{:S(2)}, u32[]{:S(2)}) collective-permute-start(bf16[512,512]{1,0:T(8,128)(2,1)S(1)} %add_convert_fusion.refs_0_), channel_id=1, source_target_pairs={{0,1},{1,0},{2,3},{3,2},{4,5},{5,4},{6,7},{7,6},{8,9},{9,8},{10,11... | collective-permute-start | bytes 1572872 | tf_op jit(solution)/shard_map/ppermute | solution.py:402
  86.7 25.0 %collective-permute-start.15 = (bf16[512,512]{1,0:T(8,128)(2,1)S(1)}, bf16[512,512]{1,0:T(8,128)(2,1)S(1)}, u32[]{:S(2)}, u32[]{:S(2)}) collective-permute-start(bf16[512,512]{1,0:T(8,128)(2,1)S(1)} %add_convert_fusion.refs_0_), channel_id=1, source_target_pairs={{0,2},{2,4},{4,6},{1,3},{3,5},{5,7},{8,10},{10,12},{12,14},{9,11},... | collective-permute-start | bytes 1572872 | tf_op jit(solution)/shard_map/ppermute | solution.py:403
  90.2 33.4 %collective-permute-start.17 = (bf16[512,512]{1,0:T(8,128)(2,1)S(1)}, bf16[512,512]{1,0:T(8,128)(2,1)}, u32[]{:S(2)}, u32[]{:S(2)}) collective-permute-start(bf16[512,512]{1,0:T(8,128)(2,1)S(1)} %add_convert_fusion.refs_0_), channel_id=1, source_target_pairs={{0,6},{1,7},{8,14},{9,15},{16,22},{17,23},{24,30},{25,31},{32,38},... | collective-permute-start | bytes 1572872 | tf_op jit(solution)/shard_map/ppermute | solution.py:404
  101.3 28.6 %collective-permute-start.20 = (bf16[512,512]{1,0:T(8,128)(2,1)S(1)}, bf16[512,512]{1,0:T(8,128)(2,1)S(1)}, u32[]{:S(2)}, u32[]{:S(2)}) collective-permute-start(bf16[512,512]{1,0:T(8,128)(2,1)S(1)} %collective-permute-done.16.refs_3_), channel_id=1, source_target_pairs={{0,1},{1,0},{2,3},{3,2},{4,5},{5,4},{6,7},{7,6},{8,9},{9,8},{10,11... | collective-permute-start | bytes 1572872 | tf_op jit(solution)/shard_map/ppermute | solution.py:409
  103.6 26.3 %collective-permute-start.21 = (bf16[512,512]{1,0:T(8,128)(2,1)S(1)}, bf16[512,512]{1,0:T(8,128)(2,1)S(1)}, u32[]{:S(2)}, u32[]{:S(2)}) collective-permute-start(bf16[512,512]{1,0:T(8,128)(2,1)S(1)} %collective-permute-done.14.refs_1_), channel_id=1, source_target_pairs={{0,6},{1,7},{8,14},{9,15},{16,22},{17,23},{24,30},{25,31},{32,38},... | collective-permute-start | bytes 1572872 | tf_op jit(solution)/shard_map/ppermute | solution.py:408
  105.0 24.9 %collective-permute-start.18 = (bf16[512,256]{1,0:T(8,128)(2,1)}, bf16[512,256]{1,0:T(8,128)(2,1)S(1)}, u32[]{:S(2)}, u32[]{:S(2)}) collective-permute-start(bf16[512,256]{1,0:T(8,128)(2,1)} %slice.8), channel_id=1, source_target_pairs={{0,2},{2,4},{4,6},{1,3},{3,5},{5,7},{8,10},{10,12},{12,14},{9,11},... | collective-permute-start | bytes 786440 | tf_op jit(solution)/shard_map/ppermute | solution.py:406
  112.5 17.4 %collective-permute-start.19 = (bf16[512,256]{1,0:T(8,128)(2,1)}, bf16[512,256]{1,0:T(8,128)(2,1)}, u32[]{:S(2)}, u32[]{:S(2)}) collective-permute-start(bf16[512,256]{1,0:T(8,128)(2,1)} %slice.9), channel_id=1, source_target_pairs={{0,1},{1,0},{2,3},{3,2},{4,5},{5,4},{6,7},{7,6},{8,9},{9,8},{10,11... | collective-permute-start | bytes 786440 | tf_op jit(solution)/shard_map/ppermute | solution.py:407
  114.8 2.2 %copy-start.1 = (bf16[1,512,4096]{2,1,0:T(8,128)(2,1)S(1)}, bf16[1,512,4096]{2,1,0:T(8,128)(2,1)}, u32[]{:S(2)}) copy-start(bf16[1,512,4096]{2,1,0:T(8,128)(2,1)} %param.9) | copy-start | bytes 12582916
  117.0 4.0 %copy-start.2 = (bf16[32,1280,128]{2,1,0:T(8,128)(2,1)S(1)}, bf16[32,1280,128]{2,1,0:T(8,128)(2,1)}, u32[]{:S(2)}) copy-start(bf16[32,1280,128]{2,1,0:T(8,128)(2,1)} %all-gather.3.cloned.1.call-done) | copy-start | bytes 31457284
  121.0 8.9 %copy-start.3 = (bf16[32,1280,128]{2,1,0:T(8,128)(2,1)S(1)}, bf16[32,1280,128]{2,1,0:T(8,128)(2,1)}, u32[]{:S(2)}) copy-start(bf16[32,1280,128]{2,1,0:T(8,128)(2,1)} %all-gather.3.cloned.1.call-done) | copy-start | bytes 31457284
Sparse Core Ops, SparseCore 0:
  30.3 69.1 all-gather.2
